TPU v7x, 512 devices: a whole 4x4x16 slice. The times are simulated.
512 devices in a mesh: lat: 16 (over z_lo, core), lon: 32 (over y, x, z_hi).
Axes of the slice: x: 4, y: 4, z: 16 (z_hi: 2, z_lo: 8; z = z_hi * 8 + z_lo), core: 2. Of those that a mesh axis runs over, the one named last changes fastest.
Arguments:
- tokens: bfloat16 [768, 1152, 512], P('lat', 'lon'), may hold values from -6 to 6
- region: int32 [768, 1152], P('lat', 'lon'), may hold values from 0 to 2
- ln_gain: float32 [512], replicated, may hold values from 0.1 to 1.9
- qkv_weight: bfloat16 [512, 1536], P('lon'), may hold values from -1.5 to 1.5
- proj_weight: bfloat16 [512, 512], P('lon'), may hold values from -0.25 to 0.25
- position_bias: float32 [16, 72, 72], replicated, may hold values from -4 to 4
Outputs:
- mixed: bfloat16 [768, 1152, 512], P('lat', 'lon')
All inputs are finite; a program needn't handle non-finite values.
Results may differ from a plain program's by a relative error of at most 0.0055.
Values may be sent and summed in bfloat16 or wider, within the bound.
A program may use at most 64 MiB of HBM per device.

v0:
```python
import math

import jax
import jax.numpy as jnp
from jax import lax
from jax.sharding import PartitionSpec as P

HEADS = 16
HD = 32
WIN_LAT = 6
WIN_LON = 12
WIN = 72
SHIFT_LAT = 3
SHIFT_LON = 6


def passed_along(block, axis, distance):
    devices = range(lax.axis_size(axis))
    route = [((i - distance) % len(devices), i) for i in devices]
    return lax.ppermute(block, axis, route)


def layer_norm(x, gain):
    xf = x.astype(jnp.float32)
    mean = jnp.mean(xf, axis=-1, keepdims=True)
    var = jnp.mean((xf - mean) ** 2, axis=-1, keepdims=True)
    return ((xf - mean) * lax.rsqrt(var + 1e-05) * gain).astype(jnp.bfloat16)


def to_windows(x, rows, cols):
    nr = rows // WIN_LAT
    nc = cols // WIN_LON
    rest = x.shape[2:]
    y = x.reshape((nr, WIN_LAT, nc, WIN_LON) + rest)
    y = jnp.moveaxis(y, 2, 1)
    return y.reshape((nr * nc, WIN) + rest)


def from_windows(y, rows, cols):
    nr = rows // WIN_LAT
    nc = cols // WIN_LON
    width = y.shape[-1]
    x = y.reshape(nr, nc, WIN_LAT, WIN_LON, width)
    x = jnp.moveaxis(x, 1, 2)
    return x.reshape(rows, cols, width)


def attend_windows(win, regw, loww, qkv_full, proj_full, position_bias):
    count = win.shape[0]
    width = win.shape[2]
    qkv = jnp.dot(
        win.reshape(count * WIN, width), qkv_full, preferred_element_type=jnp.float32
    ).astype(jnp.bfloat16)
    qkv = qkv.reshape(count, WIN, 3, HEADS, HD)
    scores = jnp.einsum(
        "gqhd,gkhd->ghqk", qkv[:, :, 0], qkv[:, :, 1], preferred_element_type=jnp.float32
    )
    scores = scores * HD ** (-0.5) + position_bias[None]
    allowed = (regw[:, :, None] == regw[:, None, :]) & (loww[:, :, None] == loww[:, None, :])
    scores = jnp.where(allowed[:, None], scores, -1e30)
    top = jnp.max(scores, axis=-1, keepdims=True)
    expo = jnp.exp(scores - top)
    probs = (expo / jnp.sum(expo, axis=-1, keepdims=True)).astype(jnp.bfloat16)
    context = jnp.einsum(
        "ghqk,gkhd->gqhd", probs, qkv[:, :, 2], preferred_element_type=jnp.float32
    ).astype(jnp.bfloat16)
    out = jnp.dot(
        context.reshape(count * WIN, width), proj_full, preferred_element_type=jnp.float32
    )
    return out.astype(jnp.bfloat16).reshape(count, WIN, width)


def local(tokens, region, ln_gain, qkv_weight, proj_weight, position_bias):
    rows, cols, width = tokens.shape
    qkv_full, proj_full = (
        lax.all_gather(qkv_weight, "lon", axis=0, tiled=True),
        lax.all_gather(proj_weight, "lon", axis=0, tiled=True),
    )
    normed = layer_norm(tokens, ln_gain)
    labels = region.astype(jnp.bfloat16)
    next_h, next_r = passed_along((normed, labels), "lat", -1)
    part_h = jnp.concatenate([normed[SHIFT_LAT:], next_h[:SHIFT_LAT]], 0)
    part_r = jnp.concatenate([labels[SHIFT_LAT:], next_r[:SHIFT_LAT]], 0)
    beside_h, beside_r = passed_along((part_h, part_r), "lon", -1)
    side_h = beside_h[:, :SHIFT_LON]
    side_r = beside_r[:, :SHIFT_LON]
    shifted = jnp.concatenate([part_h[:, SHIFT_LON:], side_h], 1)
    shifted_r = jnp.concatenate([part_r[:, SHIFT_LON:], side_r], 1)
    total_rows = rows * lax.axis_size("lat")
    global_rows = (
        lax.axis_index("lat") * rows + SHIFT_LAT + jnp.arange(rows, dtype=jnp.int32)
    ) % total_rows
    lowgrid = jnp.broadcast_to((global_rows < SHIFT_LAT).astype(jnp.int32)[:, None], (rows, cols))
    win = to_windows(shifted, rows, cols)
    regw = to_windows(shifted_r, rows, cols)
    loww = to_windows(lowgrid, rows, cols)
    count = win.shape[0]
    group = math.gcd(count, 8)
    steps_n = count // group

    def one_group(args):
        wb, rb, lb = args
        return attend_windows(wb, rb, lb, qkv_full, proj_full, position_bias)

    outs = lax.map(
        one_group,
        (
            win.reshape(steps_n, group, WIN, width),
            regw.reshape(steps_n, group, WIN),
            loww.reshape(steps_n, group, WIN),
        ),
    )
    attended = from_windows(outs.reshape(count, WIN, width), rows, cols)
    down = passed_along(attended[rows - SHIFT_LAT :], "lat", 1)
    upright = jnp.concatenate([down, attended[: rows - SHIFT_LAT]], 0)
    across = passed_along(upright[:, cols - SHIFT_LON :], "lon", 1)
    own = jnp.concatenate([across, upright[:, : cols - SHIFT_LON]], 1)
    return (tokens.astype(jnp.float32) + own.astype(jnp.float32)).astype(jnp.bfloat16)


def solution(mesh):
    return jax.shard_map(
        local,
        mesh=mesh,
        in_specs=(P("lat", "lon", None), P("lat", "lon"), P(), P("lon", None), P("lon", None), P()),
        out_specs=P("lat", "lon", None),
        check_vma=False,
    )
```

profile of v0, /device:TPU:0, one launch (start us, length us, event | category | flops | bytes accessed | tf_op | source)
XLA Modules:
  0.0 544.4 jit_solution(10057694404124381392)
XLA Ops:
  6.5 1.9 convert_reduce_fusion
  8.5 0.8 fusion.14
  9.4 0.8 fusion.16
  10.2 7.2 %collective-permute-start = (bf16[48,36,512]{2,0,1:T(8,128)(2,1)S(1)}, bf16[48,36,512]{2,0,1:T(8,128)(2,1)}, u32[]{:S(2)}, u32[]{:S(2)}) collective-permute-start(bf16[48,36,512]{2,0,1:T(8,128)(2,1)S(1)} %fusion.16), channel_id=1, source_target_pairs={{32,0},{64,32},{96,64},{128,96},{160,128},{192,160},{224,192},{256... | collective-permute-start | bytes 5308424 | tf_op jit(solution)/shard_map/ppermute | solution.py:20
  17.5 0.9 slice.60
  18.5 19.4 %collective-permute-done = bf16[48,36,512]{2,0,1:T(8,128)(2,1)} collective-permute-done((bf16[48,36,512]{2,0,1:T(8,128)(2,1)S(1)}, bf16[48,36,512]{2,0,1:T(8,128)(2,1)}, u32[]{:S(2)}, u32[]{:S(2)}) %collective-permute-start) | collective-permute-done | bytes 1769504 | tf_op jit(solution)/shard_map/ppermute | solution.py:20
  37.8 1.0 slice.61
  39.1 12.6 %collective-permute-start.1 = (bf16[48,36,512]{2,0,1:T(8,128)(2,1)S(1)}, bf16[48,36,512]{2,0,1:T(8,128)(2,1)}, u32[]{:S(2)}, u32[]{:S(2)}) collective-permute-start(bf16[48,36,512]{2,0,1:T(8,128)(2,1)S(1)} %pad_maximum_fusion), channel_id=1, source_target_pairs={{1,0},{2,1},{3,2},{4,3},{5,4},{6,5},{7,6},{8,7},{9,8},{10,9},{11,1... | collective-permute-start | bytes 5308424 | tf_op jit(solution)/shard_map/ppermute | solution.py:20
  52.3 10.5 %collective-permute-start.2 = (bf16[48,36]{0,1:T(8,128)(2,1)}, bf16[48,36]{0,1:T(8,128)(2,1)}, u32[]{:S(2)}, u32[]{:S(2)}) collective-permute-start(bf16[48,36]{0,1:T(8,128)(2,1)} %convert_element_type.40), channel_id=1, source_target_pairs={{32,0},{64,32},{96,64},{128,96},{160,128},{192,160},{224,192},{256... | collective-permute-start | bytes 10376 | tf_op jit(solution)/shard_map/ppermute | solution.py:20
  62.8 321.8 %all_gather.7 = bf16[512,512]{1,0:T(8,128)(2,1)} all-gather(bf16[16,512]{1,0:T(8,128)(2,1)S(1)} %copy-done.6), channel_id=1, replica_groups=mesh['lat'=16,'lon'=32] {'lon'}, dimensions={0}, use_global_device_ids=true | all-gather | bytes 540672 | tf_op jit(solution)/shard_map/all_gather | solution.py:77
  384.6 0.8 slice.65
  385.4 2.1 copy.24
  387.5 0.7 transpose.30
  388.2 1.6 reshape_reshape.14
  389.8 0.8 pad_maximum_fusion.5
  390.5 2.1 collective-permute-start.3
  392.6 0.8 fusion.20
  393.4 11.4 %collective-permute-done.3 = bf16[48,36]{0,1:T(8,128)(2,1)S(1)} collective-permute-done((bf16[48,36]{0,1:T(8,128)(2,1)S(1)}, bf16[48,36]{0,1:T(8,128)(2,1)S(1)}, u32[]{:S(2)}, u32[]{:S(2)}) %collective-permute-start.3) | collective-permute-done | bytes 3488 | tf_op jit(solution)/shard_map/ppermute | solution.py:20
  405.4 0.8 copy.22
  406.2 0.7 reshape.67
  406.9 1.4 copy.23
  408.3 0.9 reshape_reshape.13
  409.2 1.1 fusion.19
  410.3 1.0 slice.64
  411.3 1.4 pad_maximum_fusion.2
  412.7 2.5 reshape.66
  415.3 2.5 copy.21
  417.7 3.8 reshape_reshape.12
  421.6 56.7 %while.10 = (s32[]{:T(128)}, bf16[3,8,72,512]{3,2,1,0:T(8,128)(2,1)}, bf16[3,8,72,512]{3,2,1,0:T(8,128)(2,1)}, bf16[512,1536]{1,0:T(8,128)(2,1)}, bf16[3,8,72]{2...) while((s32[]{:T(128)}, ...), condition=%wide.region_5.6_spmd, body=%wide.region_2.5_spmd.sunk | while | flops 1301211648 | bytes 37871392 | solution.py:105
  421.6 1.1 constant_dynamic-slice_fusion.2
  422.7 2.5 convolution_convert_fusion.4
  425.2 2.3 copy.44
  427.4 5.0 reshape.71
  432.7 1.4 fusion.45
  435.1 1.7 fusion.46
  436.8 0.8 fusion.47
  438.3 0.8 reshape.72
  439.6 0.9 constant_dynamic-update-slice_fusion.2
  440.5 1.1 constant_dynamic-slice_fusion.2
  441.6 2.5 convolution_convert_fusion.4
  444.1 2.3 copy.44
  446.4 5.0 reshape.71
  451.6 1.4 fusion.45
  454.0 1.7 fusion.46
  455.7 0.8 fusion.47
  457.2 0.8 reshape.72
  458.5 0.9 constant_dynamic-update-slice_fusion.2
  459.4 1.1 constant_dynamic-slice_fusion.2
  460.5 2.5 convolution_convert_fusion.4
  463.0 2.3 copy.44
  465.3 5.0 reshape.71
  470.5 1.4 fusion.45
  472.9 1.7 fusion.46
  474.6 0.8 fusion.47
  476.1 0.8 reshape.72
  477.4 0.9 constant_dynamic-update-slice_fusion.2
  478.3 2.4 reshape_reshape.15
  480.7 2.4 copy.25
  483.2 2.8 reshape.68
  486.0 1.9 collective-permute-start.4
  488.0 25.9 %collective-permute-done.4 = bf16[3,36,512]{2,0,1:T(4,128)(2,1)S(1)} collective-permute-done((bf16[3,36,512]{2,0,1:T(4,128)(2,1)S(1)}, bf16[3,36,512]{2,0,1:T(4,128)(2,1)S(1)}, u32[]{:S(2)}, u32[]{:S(2)}) %collective-permute-start.4) | collective-permute-done | bytes 110624 | tf_op jit(solution)/shard_map/ppermute | solution.py:20
  513.9 1.9 collective-permute-start.5
  515.9 19.6 %collective-permute-done.5 = bf16[48,6,512]{2,0,1:T(8,128)(2,1)S(1)} collective-permute-done((bf16[48,6,512]{2,0,1:T(8,128)(2,1)S(1)}, bf16[48,6,512]{2,0,1:T(8,128)(2,1)S(1)}, u32[]{:S(2)}, u32[]{:S(2)}) %collective-permute-start.5) | collective-permute-done | bytes 294944 | tf_op jit(solution)/shard_map/ppermute | solution.py:20
  535.5 2.1 fusion.17
  (57 shorter events, 8.7 us)
Async XLA Ops:
  6.5 2.0 copy-start
  6.5 2.8 copy-start.7
  6.5 415.0 %all-gather.2.cloned.1.call-start = ((), (), s32[]{:S(2)}) async-start(), calls=%async_computation | async-start | bytes 1622016 | tf_op jit(solution)/shard_map/all_gather | solution.py:76
  10.2 27.6 %collective-permute-start = (bf16[48,36,512]{2,0,1:T(8,128)(2,1)S(1)}, bf16[48,36,512]{2,0,1:T(8,128)(2,1)}, u32[]{:S(2)}, u32[]{:S(2)}) collective-permute-start(bf16[48,36,512]{2,0,1:T(8,128)(2,1)S(1)} %fusion.16), channel_id=1, source_target_pairs={{32,0},{64,32},{96,64},{128,96},{160,128},{192,160},{224,192},{256... | collective-permute-start | bytes 5308424 | tf_op jit(solution)/shard_map/ppermute | solution.py:20
  18.4 33.2 %copy-start.5 = (s32[48,36]{0,1:T(8,128)S(1)}, s32[48,36]{0,1:T(8,128)}, u32[]{:S(2)}) copy-start(s32[48,36]{0,1:T(8,128)} %param.9) | copy-start | bytes 20740
  18.5 44.4 %copy-start.6 = (bf16[16,512]{1,0:T(8,128)(2,1)S(1)}, bf16[16,512]{1,0:T(8,128)(2,1)}, u32[]{:S(2)}) copy-start(bf16[16,512]{1,0:T(8,128)(2,1)} %param.12) | copy-start | bytes 49156
  38.8 12.8 %copy-start.2 = (bf16[3,36,512]{2,0,1:T(4,128)(2,1)}, bf16[3,36,512]{2,0,1:T(4,128)(2,1)S(1)}, u32[]{:S(2)}) copy-start(bf16[3,36,512]{2,0,1:T(4,128)(2,1)S(1)} %slice.61) | copy-start | bytes 331780
  39.1 371.2 %collective-permute-start.1 = (bf16[48,36,512]{2,0,1:T(8,128)(2,1)S(1)}, bf16[48,36,512]{2,0,1:T(8,128)(2,1)}, u32[]{:S(2)}, u32[]{:S(2)}) collective-permute-start(bf16[48,36,512]{2,0,1:T(8,128)(2,1)S(1)} %pad_maximum_fusion), channel_id=1, source_target_pairs={{1,0},{2,1},{3,2},{4,3},{5,4},{6,5},{7,6},{8,7},{9,8},{10,9},{11,1... | collective-permute-start | bytes 5308424 | tf_op jit(solution)/shard_map/ppermute | solution.py:20
  52.3 337.5 %collective-permute-start.2 = (bf16[48,36]{0,1:T(8,128)(2,1)}, bf16[48,36]{0,1:T(8,128)(2,1)}, u32[]{:S(2)}, u32[]{:S(2)}) collective-permute-start(bf16[48,36]{0,1:T(8,128)(2,1)} %convert_element_type.40), channel_id=1, source_target_pairs={{32,0},{64,32},{96,64},{128,96},{160,128},{192,160},{224,192},{256... | collective-permute-start | bytes 10376 | tf_op jit(solution)/shard_map/ppermute | solution.py:20
  390.5 14.3 %collective-permute-start.3 = (bf16[48,36]{0,1:T(8,128)(2,1)S(1)}, bf16[48,36]{0,1:T(8,128)(2,1)S(1)}, u32[]{:S(2)}, u32[]{:S(2)}) collective-permute-start(bf16[48,36]{0,1:T(8,128)(2,1)S(1)} %pad_maximum_fusion.5), channel_id=1, source_target_pairs={{1,0},{2,1},{3,2},{4,3},{5,4},{6,5},{7,6},{8,7},{9,8},{10,9},{11,1... | collective-permute-start | bytes 10376 | tf_op jit(solution)/shard_map/ppermute | solution.py:20
  432.7 2.3 copy-start.3
  437.6 1.5 copy-start.4
  451.6 2.4 copy-start.3
  456.5 1.5 copy-start.4
  470.5 2.3 copy-start.3
  475.4 1.5 copy-start.4
  483.2 52.3 %copy-start.1 = (bf16[48,36,512]{2,0,1:T(8,128)(2,1)S(1)}, bf16[48,36,512]{2,0,1:T(8,128)(2,1)}, u32[]{:S(2)}) copy-start(bf16[48,36,512]{2,0,1:T(8,128)(2,1)} %param.8) | copy-start | bytes 5308420
  486.0 27.8 %collective-permute-start.4 = (bf16[3,36,512]{2,0,1:T(4,128)(2,1)S(1)}, bf16[3,36,512]{2,0,1:T(4,128)(2,1)S(1)}, u32[]{:S(2)}, u32[]{:S(2)}) collective-permute-start(bf16[3,36,512]{2,0,1:T(4,128)(2,1)S(1)} %slice.70), channel_id=1, source_target_pairs={{480,0},{0,32},{32,64},{64,96},{96,128},{128,160},{160,192},{192,2... | collective-permute-start | bytes 331784 | tf_op jit(solution)/shard_map/ppermute | solution.py:20
  513.9 21.5 %collective-permute-start.5 = (bf16[48,6,512]{2,0,1:T(8,128)(2,1)S(1)}, bf16[48,6,512]{2,0,1:T(8,128)(2,1)S(1)}, u32[]{:S(2)}, u32[]{:S(2)}) collective-permute-start(bf16[48,6,512]{2,0,1:T(8,128)(2,1)S(1)} %pad_maximum_fusion.3), channel_id=1, source_target_pairs={{31,0},{0,1},{1,2},{2,3},{3,4},{4,5},{5,6},{6,7},{7,8},{8,9},{9,10... | collective-permute-start | bytes 884744 | tf_op jit(solution)/shard_map/ppermute | solution.py:20
Sparse Core Ops, SparseCore 0:
  17.6 224.4 all-gather.1
where the time goes:
time: 546 us; the launch traced here: 544 us
  blocking collectives  322 us (59%)
  waiting for transfers between devices  76.3 us (14%)
  local copies, waits for them, and re-layouts  63.6 us (12%)
  starting transfers between devices  36.2 us (7%)
  other arithmetic  17.1 us (3%)
  matrix products  15.5 us (3%)
  between operations  13.6 us (2%)
    all_gather x1, blocking collectives, local(): lax.all_gather(proj_weight, 'lon', axis=0, tiled=True)  322 us
    ppermute x6, waiting for transfers between devices, passed_along(): return lax.ppermute(block, axis, route)  76.3 us
    ppermute x6, starting transfers between devices, passed_along(): return lax.ppermute(block, axis, route)  36.2 us
    reshape x3, local copies, waits for them, and re-layouts, attend_windows(): qkv = qkv.reshape(count, WIN, 3, HEADS, HD)  15.1 us
  transfers between devices with their start and end apart: 7, of which 4 were waited for; matrix products, arithmetic and copies ran while one was open for 5% of the time, Pallas kernels for 0%

commit v1 on v0

v1 whole, which is shorter than its diff:
```python
import functools
import math

import jax
import jax.numpy as jnp
from jax import lax
from jax.experimental import pallas as pl
from jax.experimental.pallas import tpu as pltpu
from jax.sharding import PartitionSpec as P

HEADS = 16
HD = 32
C = 512
WIN = 72
ROWS = 48
COLS = 36
EXT = 48
FEAT = 128
WIDE = C + FEAT
LOG2E = math.log2(math.e)
SCALE = HD**-0.5 * LOG2E
MASKED = -1e30
UNITS = 18
BF = jnp.bfloat16
F32 = jnp.float32
I32 = jnp.int32
MESH = pl.DeviceIdType.MESH
NT = (((1,), (1,)), ((), ()))


def dot(a, b):
    return jnp.dot(a, b, preferred_element_type=F32)


def dot_nt(a, b, precision=None):
    return lax.dot_general(a, b, NT, preferred_element_type=F32, precision=precision)


def token_parts(t):
    half = (t >= 36).astype(I32)
    u = t - 36 * half
    c = (u * 43) >> 7
    return half, c, u - 3 * c


def block_place(t):
    half, c, r = token_parts(t)
    return c * 16 + half * 3 + r


def normed_rows(x, gain):
    mean = jnp.sum(x, axis=-1, keepdims=True) * (1.0 / C)
    d = x - mean
    var = jnp.sum(d * d, axis=-1, keepdims=True) * (1.0 / C)
    return (d * lax.rsqrt(var + 1e-05) * gain).astype(BF).astype(F32)


def kernel(
    nlat,
    nlon,
    tok,
    reg,
    gain_hbm,
    wqkv,
    wproj,
    bias_hbm,
    out,
    xo,
    halo,
    relay,
    lab_own,
    lab_send,
    lab_recv,
    lab_ext,
    lab_t,
    gain,
    bias_raw,
    bias,
    wbuf,
    wvt,
    wpt,
    xn,
    acc,
    xwin,
    pk_top,
    pk_bot,
    qk,
    vt,
    ctx,
    loc_sem,
    out_sem,
    z_send,
    z_recv,
    own_send,
    own_recv,
    par_send,
    par_recv,
    sib_send,
    sib_recv,
    leg_send,
    leg_recv,
    halo_send,
    halo_recv,
    lab_ssem,
    lab_rsem,
    lat_send,
    lat_recv,
):
    shard = C // nlon
    plane = nlon // 2
    lat = lax.axis_index("lat")
    lon = lax.axis_index("lon")
    core = lax.rem(lat, 2)
    zhi = lax.rem(lon, 2)
    m = lon // 2
    lat_up = lax.rem(lat + 1, nlat)
    lat_dn = lax.rem(lat + nlat - 1, nlat)
    lon_up = lax.rem(lon + 1, nlon)
    lon_dn = lax.rem(lon + nlon - 1, nlon)
    lon_pair = lon + 1 - 2 * zhi
    lat_mirror = (nlat // 2 - 1 - lat // 2) * 2 + core
    lat_sib = lat + 1 - 2 * core

    zlo = nlat // 2
    ring = 2 * zlo
    leg = zlo // 2
    z = zhi * zlo + lat // 2

    def chip_at(column, place):
        place = lax.rem(place + 2 * ring, ring)
        return lax.rem(place, zlo) * 2 + core, column * 2 + place // zlo

    above = chip_at(m, z + leg)
    below = chip_at(m, z - leg)

    def beyond(place, by):
        lat_s, lon_s = chip_at(m, place)
        return lat_s, lax.rem(lon_s + by + nlon, nlon)

    onward = (beyond(z - leg, 1), beyond(z + leg, -1))
    relays_here = (
        chip_at(lon_dn // 2, lax.rem(lon_dn, 2) * zlo + lat // 2 + leg),
        chip_at(lon_up // 2, lax.rem(lon_up, 2) * zlo + lat // 2 - leg),
    )

    loads = [
        pltpu.make_async_copy(wqkv.at[:, 0:1024], wbuf.at[0, pl.ds(lon * shard, shard), :], loc_sem.at[0]),
        pltpu.make_async_copy(
            wqkv.at[:, 1024:1536], wbuf.at[1, pl.ds(lon * shard, shard), 0:512], loc_sem.at[1]
        ),
        pltpu.make_async_copy(wproj, wbuf.at[1, pl.ds(lon * shard, shard), 512:1024], loc_sem.at[2]),
        pltpu.make_async_copy(reg, lab_own, loc_sem.at[3]),
        pltpu.make_async_copy(tok, xo, loc_sem.at[4]),
        pltpu.make_async_copy(gain_hbm, gain, loc_sem.at[5]),
        pltpu.make_async_copy(bias_hbm, bias_raw, loc_sem.at[6]),
    ]
    for copy in loads:
        copy.start()

    barrier = pltpu.get_barrier_semaphore()
    greeted = (
        (lat, lon_up),
        (lat, lon_dn),
        (lat_up, lon),
        (lat_dn, lon),
        (lat_mirror, lon_pair),
        above,
        below,
    )
    greeted = greeted + relays_here
    for there in greeted:
        pl.semaphore_signal(barrier, inc=1, device_id=there, device_id_type=MESH)

    def greet(d, carry):
        pl.semaphore_signal(
            barrier,
            inc=1,
            device_id=(lat, lax.rem(m + d, plane) * 2 + zhi),
            device_id_type=MESH,
        )
        return carry

    lax.fori_loop(1, plane, greet, 0)
    pl.semaphore_wait(barrier, len(greeted) + plane - 1)

    def mirror_copy(rows_of):
        rows = pl.ds(rows_of * shard, shard)
        return pltpu.make_async_remote_copy(
            src_ref=wbuf.at[core, rows, :],
            dst_ref=wbuf.at[core, rows, :],
            send_sem=z_send,
            recv_sem=z_recv,
            device_id=(lat_mirror, lon_pair),
            device_id_type=MESH,
        )

    def plane_copy(rows_of, other, mark, send, recv):
        rows = pl.ds(rows_of * shard, shard)
        return pltpu.make_async_remote_copy(
            src_ref=wbuf.at[core, rows, :],
            dst_ref=wbuf.at[core, rows, :],
            send_sem=send,
            recv_sem=recv.at[mark],
            device_id=(lat, other * 2 + zhi),
            device_id_type=MESH,
        )

    def sibling_copy(half, owner):
        rows = pl.ds(owner * 2 * shard, 2 * shard)
        return pltpu.make_async_remote_copy(
            src_ref=wbuf.at[half, rows, :],
            dst_ref=wbuf.at[half, rows, :],
            send_sem=sib_send.at[owner],
            recv_sem=sib_recv.at[owner],
            device_id=(lat_sib, lon),
            device_id_type=MESH,
        )

    def sibling_pair_copy(half):
        rows = pl.ds(lon_pair * shard, shard)
        return pltpu.make_async_remote_copy(
            src_ref=wbuf.at[half, rows, :],
            dst_ref=wbuf.at[half, rows, :],
            send_sem=sib_send.at[m],
            recv_sem=sib_recv.at[m],
            device_id=(lat_sib, lon),
            device_id_type=MESH,
        )

    for k in range(3):
        loads[k].wait()
    mirror_copy(lon).start()

    def send_own(d, carry):
        plane_copy(lon, lax.rem(m + d, plane), m, own_send.at[d], own_recv).start()
        return carry

    lax.fori_loop(1, plane, send_own, 0)

    def leg_copy(side, k):
        rows = pl.ds((0, 32, 16)[k], 16)
        cols = pl.ds(COLS - 6, 6) if side == 0 else pl.ds(0, 6)
        return pltpu.make_async_remote_copy(
            src_ref=tok.at[cols, rows, :],
            dst_ref=relay.at[side, :, rows, :],
            send_sem=leg_send.at[side, k],
            recv_sem=leg_recv.at[side, k],
            device_id=(above, below)[side],
            device_id_type=MESH,
        )

    def halo_copy(side, k):
        rows = pl.ds((0, 32, 16)[k], 16)
        return pltpu.make_async_remote_copy(
            src_ref=relay.at[side, :, rows, :],
            dst_ref=halo.at[side, :, rows, :],
            send_sem=halo_send.at[side, k],
            recv_sem=halo_recv.at[side, k],
            device_id=onward[side],
            device_id_type=MESH,
        )

    def set_out(k):
        for side in range(2):
            leg_copy(side, k).start()

    def forward(k):
        for side in range(2):
            leg_copy(side, k).wait_recv()
            halo_copy(side, k).start()

    def label_copy(side):
        return pltpu.make_async_remote_copy(
            src_ref=lab_send.at[side],
            dst_ref=lab_recv.at[side],
            send_sem=lab_ssem.at[side],
            recv_sem=lab_rsem.at[side],
            device_id=(lat, lon_up if side == 0 else lon_dn),
            device_id_type=MESH,
        )

    loads[3].wait()
    lab_send[...] = jnp.zeros_like(lab_send)
    lab_send[0, 0:6, 0:ROWS] = lab_own[COLS - 6 : COLS, :]
    lab_send[1, 0:6, 0:ROWS] = lab_own[0:6, :]
    for side in range(2):
        label_copy(side).start()
    set_out(0)

    mirror_copy(lon_pair).wait_recv()

    def send_pair(d, carry):
        plane_copy(lon_pair, lax.rem(m + d, plane), m, par_send.at[d], par_recv).start()
        return carry

    lax.fori_loop(1, plane, send_pair, 0)
    sibling_pair_copy(core).start()

    loads[4].wait()
    loads[5].wait()
    loads[6].wait()

    def own_column(c, carry):
        x = xo[c].astype(F32)
        acc[c + 6] = x
        xn[c + 6, :, 0:C] = normed_rows(x, gain[...])
        return carry

    lax.fori_loop(0, COLS, own_column, 0)

    def place_rows(count):
        half, c, r = token_parts(lax.broadcasted_iota(I32, (count, WIN), 0))
        place = jnp.where(
            lax.broadcasted_iota(I32, (count, WIN), 0) < WIN, (half * 3 + r) * 12 + c, -1
        )
        return (lax.broadcasted_iota(I32, (count, WIN), 1) == place).astype(F32)

    def bias_of(h, carry):
        keys_first = dot_nt(place_rows(WIN), bias_raw[h], lax.Precision.HIGHEST)
        bias[h] = dot_nt(keys_first, place_rows(128), lax.Precision.HIGHEST) * LOG2E
        return carry

    lax.fori_loop(0, HEADS, bias_of, 0)
    ctx[...] = jnp.zeros_like(ctx)

    for side in range(2):
        label_copy(side).wait_recv()
    lab_ext[0:6, :] = lab_recv[0, 0:6, 0:ROWS]
    lab_ext[6 : 6 + COLS, :] = lab_own[...]
    lab_ext[6 + COLS : EXT, :] = lab_recv[1, 0:6, 0:ROWS]
    eye = (
        lax.broadcasted_iota(I32, (ROWS, ROWS), 0) == lax.broadcasted_iota(I32, (ROWS, ROWS), 1)
    ).astype(BF)
    low = ((lax.broadcasted_iota(I32, (ROWS, EXT), 0) < 3) & (lat == 0)).astype(F32)
    lab_t[...] = dot_nt(eye, lab_ext[...].astype(F32).astype(BF)) + 3.0 * low

    def features(e, carry):
        lane = lax.broadcasted_iota(I32, (ROWS, EXT), 1)
        code = jnp.sum(jnp.where(lane == e, lab_t[...], 0.0), axis=1, keepdims=True)
        wide = lax.broadcasted_iota(I32, (ROWS, FEAT), 1).astype(F32)
        xn[e, :, C:WIDE] = (wide == code).astype(F32)
        return carry

    lax.fori_loop(0, EXT, features, 0)
    set_out(1)
    forward(0)

    def start_and_offset(i):
        start = 8 * ((13 * i) // 16)
        return start, 3 + 6 * i - start

    def gather(i, j, u, w):
        start, offset = start_and_offset(i)
        start = pl.multiple_of(start, 8)
        block = xn[pl.ds(12 * j, 12), pl.ds(start, 16), :].reshape(192, WIDE).astype(BF)
        t = lax.broadcasted_iota(I32, (128, 192), 0)
        place = jnp.where(t < WIN, block_place(t), -1000) + offset
        select = (lax.broadcasted_iota(I32, (128, 192), 1) == place).astype(F32).astype(BF)
        xwin[u, 128 * w : 128 * w + 128, :] = dot(select, block).astype(BF)

    def gather_inner(i, carry):
        gather(i, 1, i, 0)
        gather(i, 2, i, 1)
        return carry

    lax.fori_loop(0, 7, gather_inner, 0)

    def pass_on(d, carry):
        source = lax.rem(m + d, plane)
        plane_copy(source * 2 + zhi, source, source, own_send.at[d], own_recv).wait_recv()
        plane_copy(source * 2 + 1 - zhi, source, source, par_send.at[d], par_recv).wait_recv()
        sibling_copy(core, source).start()
        return carry

    lax.fori_loop(1, plane, pass_on, 0)

    def await_sibling(d, carry):
        sibling_copy(1 - core, lax.rem(m + d, plane)).wait_recv()
        return carry

    sibling_pair_copy(1 - core).wait_recv()
    lax.fori_loop(1, plane, await_sibling, 0)
    set_out(2)
    forward(1)
    eye_c = (
        lax.broadcasted_iota(I32, (C, C), 0) == lax.broadcasted_iota(I32, (C, C), 1)
    ).astype(F32).astype(BF)
    wvt[...] = dot_nt(eye_c, wbuf[1, :, 0:512]).astype(BF)
    wpt[...] = dot_nt(eye_c, wbuf[1, :, 512:1024]).astype(BF)

    def halo_chunk(k):
        row = (0, 32, 16)[k]
        for side in range(2):
            halo_copy(side, k).wait_recv()

        def one(c, carry):
            for side in range(2):
                x = halo[side, c, row : row + 16, :].astype(F32)
                xn[c + side * (EXT - 6), row : row + 16, 0:C] = normed_rows(x, gain[...])
            return carry

        lax.fori_loop(0, 6, one, 0)

    def pack(row, offset):
        block = xn[:, row : row + 16, :].reshape(EXT * 16, WIDE).astype(BF)
        u = lax.broadcasted_iota(I32, (144, EXT * 16), 0)
        c = (u * 171) >> 9
        place = c * 16 + (u - 3 * c) + offset
        select = (lax.broadcasted_iota(I32, (144, EXT * 16), 1) == place).astype(F32).astype(BF)
        return dot(select, block).astype(BF)

    def lat_copy(up):
        if up:
            return pltpu.make_async_remote_copy(
                src_ref=pk_bot.at[0:144],
                dst_ref=pk_top.at[0:144],
                send_sem=lat_send.at[0],
                recv_sem=lat_recv.at[0],
                device_id=(lat_up, lon),
                device_id_type=MESH,
            )
        return pltpu.make_async_remote_copy(
            src_ref=pk_top.at[144:288],
            dst_ref=pk_bot.at[144:288],
            send_sem=lat_send.at[1],
            recv_sem=lat_recv.at[1],
            device_id=(lat_dn, lon),
            device_id_type=MESH,
        )

    def gather_edges():
        t = lax.broadcasted_iota(I32, (128, 288), 0)
        lane = lax.broadcasted_iota(I32, (128, 288), 1)
        place = jnp.where(t < WIN, t + 108 * (t >= 36).astype(I32), -1000)
        for j in range(4):
            select = (lane == place + 36 * j).astype(F32).astype(BF)
            for k, rows in enumerate((pk_top, pk_bot)):
                xwin[11 + 2 * k + j // 2, 128 * (j % 2) : 128 * (j % 2) + 128, :] = dot(
                    select, rows[...]
                ).astype(BF)

    lane128 = lax.broadcasted_iota(I32, (80, 128), 1)

    def attend(u):
        first = xwin[u, 0:80, :]
        second = xwin[u, 128:208, :]
        both = jnp.concatenate([first[:, 0:C], second[:, 0:C]], axis=0)
        qk[...] = dot(both, wbuf[0]).astype(BF)
        vt[...] = dot_nt(wvt[...], xwin[u, :, 0:C]).astype(BF)
        for w in range(2):
            hot = (first, second)[w][:, C:WIDE]
            differs = jnp.where(lane128 < 6, MASKED * (1.0 - hot.astype(F32)), 0.0).astype(BF)
            for g in range(4):
                query = qk[80 * w : 80 * w + 80, 128 * g : 128 * g + 128]
                key = qk[80 * w : 80 * w + 80, 512 + 128 * g : 640 + 128 * g]
                stacked = jnp.concatenate(
                    [
                        jnp.concatenate(
                            [
                                jnp.where(lane128 // HD == k, key, jnp.zeros_like(key)),
                                hot,
                            ],
                            axis=1,
                        )
                        for k in range(4)
                    ],
                    axis=0,
                )
                scores = dot_nt(stacked, jnp.concatenate([query, differs], axis=1))
                for k in range(4):
                    h = 4 * g + k
                    s = scores[80 * k : 80 * k + WIN] * SCALE + bias[h, :, 0:80]
                    e = jnp.exp2(s - jnp.max(s, axis=0, keepdims=True))
                    total = jnp.sum(e, axis=0, keepdims=True)
                    probs = jnp.concatenate([e, jnp.zeros((8, 80), F32)], axis=0).astype(BF)
                    part = dot(vt[HD * h : HD * h + HD, 128 * w : 128 * w + 80], probs)
                    ctx[HD * h : HD * h + HD, 128 * w : 128 * w + 80] = (part * (1.0 / total)).astype(BF)
        return dot(wpt[...], ctx[...]).astype(BF)

    def unit(u, carry):
        @pl.when(u == 2)
        def _():
            forward(2)

        @pl.when(u == 7)
        def _():
            halo_chunk(0)
            pk_top[144:288, :] = pack(0, 0)
            lat_copy(False).start()
            for n in range(2):
                gather(n, 0, 7 + n, 0)
                gather(n, 3, 7 + n, 1)

        @pl.when(u == 9)
        def _():
            halo_chunk(1)
            pk_bot[0:144, :] = pack(32, 13)
            lat_copy(True).start()
            for n in range(2):
                gather(5 + n, 0, 9 + n, 0)
                gather(5 + n, 3, 9 + n, 1)

        @pl.when(u == 11)
        def _():
            lat_copy(True).wait_recv()
            lat_copy(False).wait_recv()
            gather_edges()

        @pl.when(u == 15)
        def _():
            halo_chunk(2)
            for n in range(3):
                gather(2 + n, 0, 15 + n, 0)
                gather(2 + n, 3, 15 + n, 1)

        att = attend(u)
        inner = u < 7
        edge = (u >= 11) & (u < 15)
        top = edge & (u < 13)
        bottom = edge & (u >= 13)
        i = jnp.where(inner, u, jnp.where(u < 9, u - 7, jnp.where(u < 11, u - 4, u - 13)))
        start, offset = start_and_offset(i)
        start = jnp.where(edge, jnp.where(top, 0, 32), start)
        offset = jnp.where(edge, jnp.where(top, -3, 13), offset)
        least = jnp.where(top, 36, 0)
        most = jnp.where(bottom, 36, WIN)
        start = pl.multiple_of(start, 8)
        t = lax.broadcasted_iota(I32, (192, 80), 1)
        place = jnp.where((t >= least) & (t < most), block_place(t) + offset, -1000)
        select = (lax.broadcasted_iota(I32, (192, 80), 0) == place).astype(F32).astype(BF)
        for w in range(2):
            j = jnp.where(inner, 1 + w, jnp.where(edge, 2 * ((u - 11) % 2) + w, 3 * w))
            back = dot_nt(select, att[:, 128 * w : 128 * w + 80])
            spot = (pl.ds(12 * j, 12), pl.ds(start, 16), slice(None))
            acc[spot] = acc[spot] + back.reshape(12, 16, C)
        return carry

    lax.fori_loop(0, UNITS, unit, 0)

    def finish(c, carry):
        xo[c] = acc[c + 6].astype(BF)
        return carry

    lax.fori_loop(0, COLS, finish, 0)
    store = pltpu.make_async_copy(xo, out, out_sem)
    store.start()

    mirror_copy(lon).wait_send()

    def sent(d, carry):
        plane_copy(lon, lax.rem(m + d, plane), m, own_send.at[d], own_recv).wait_send()
        plane_copy(lon_pair, lax.rem(m + d, plane), m, par_send.at[d], par_recv).wait_send()
        return carry

    lax.fori_loop(1, plane, sent, 0)

    def sent_on(d, carry):
        sibling_copy(core, lax.rem(m + d, plane)).wait_send()
        return carry

    sibling_pair_copy(core).wait_send()
    lax.fori_loop(1, plane, sent_on, 0)
    for side in range(2):
        label_copy(side).wait_send()
        for k in range(3):
            leg_copy(side, k).wait_send()
            halo_copy(side, k).wait_send()
    lat_copy(True).wait_send()
    lat_copy(False).wait_send()
    store.wait()


def local(tokens, region, ln_gain, qkv_weight, proj_weight, position_bias):
    nlat = lax.axis_size("lat")
    nlon = lax.axis_size("lon")
    plane = nlon // 2
    dma = pltpu.SemaphoreType.DMA
    vm = pltpu.VMEM
    mixed = pl.pallas_call(
        functools.partial(kernel, nlat, nlon),
        out_shape=jax.ShapeDtypeStruct((COLS, ROWS, C), BF),
        in_specs=[pl.BlockSpec(memory_space=pl.ANY)] * 6,
        out_specs=pl.BlockSpec(memory_space=pl.ANY),
        scratch_shapes=[
            vm((COLS, ROWS, C), BF),
            vm((2, 6, ROWS, C), BF),
            vm((2, 6, ROWS, C), BF),
            vm((COLS, ROWS), I32),
            vm((2, 8, 128), I32),
            vm((2, 8, 128), I32),
            vm((EXT, ROWS), I32),
            vm((ROWS, EXT), F32),
            vm((1, C), F32),
            vm((HEADS, WIN, WIN), F32),
            vm((HEADS, WIN, 128), F32),
            vm((2, C, 1024), BF),
            vm((C, C), BF),
            vm((C, C), BF),
            vm((EXT, ROWS, WIDE), F32),
            vm((EXT, ROWS, C), F32),
            vm((UNITS, 256, WIDE), BF),
            vm((288, WIDE), BF),
            vm((288, WIDE), BF),
            vm((160, 1024), BF),
            vm((C, 256), BF),
            vm((C, 256), BF),
            dma((7,)),
            dma,
            dma,
            dma,
            dma((plane,)),
            dma((plane,)),
            dma((plane,)),
            dma((plane,)),
            dma((plane,)),
            dma((plane,)),
            dma((2, 3)),
            dma((2, 3)),
            dma((2, 3)),
            dma((2, 3)),
            dma((2,)),
            dma((2,)),
            dma((2,)),
            dma((2,)),
        ],
        compiler_params=pltpu.CompilerParams(
            collective_id=0, has_side_effects=True, vmem_limit_bytes=56 * 2**20
        ),
        cost_estimate=pl.CostEstimate(
            flops=8_000_000_000, bytes_accessed=12_000_000, transcendentals=6_000_000
        ),
    )(
        jnp.transpose(tokens, (1, 0, 2)),
        jnp.transpose(region, (1, 0)),
        ln_gain.reshape(1, C),
        qkv_weight,
        proj_weight,
        position_bias,
    )
    return jnp.transpose(mixed, (1, 0, 2))


def solution(mesh):
    return jax.shard_map(
        local,
        mesh=mesh,
        in_specs=(P("lat", "lon", None), P("lat", "lon"), P(), P("lon", None), P("lon", None), P()),
        out_specs=P("lat", "lon", None),
        check_vma=False,
    )
```

time: 546 us -> 145 us (0.27)
  the two profiles are of different devices: /device:TPU:0 before, /device:TPU:24 now
where the time goes in v1:
time: 145 us
  Pallas kernels  142 us (98%)
  local copies, waits for them, and re-layouts  2.8 us (2%)
    pallas_call x1, Pallas kernels, local(): pl.pallas_call(functools.partial(kernel, nlat, nlon), out_shape=jax.Shape...  142 us

profile of v1, /device:TPU:24, one launch (start us, length us, event | category | flops | bytes accessed | tf_op | source)
XLA Modules:
  0.0 144.8 jit_solution(18067340422324499967)
XLA Ops:
  0.0 142.0 %shard_map.64 = bf16[36,48,512]{2,1,0:T(8,128)(2,1)} custom-call(bf16[36,48,512]{2,1,0:T(8,128)(2,1)} %bitcast.5, s32[36,48]{1,0:T(8,128)} %bitcast.6, f32[1,512]{1,0:T(1,128)} %bitcast.7, bf16[16,1536]{1,0:T(8,128)(2,1)} %wqkv.1, bf16[16,512]{1,0:T(8,128)(2,1)} %wproj.1, f32[16,72,72]{2,1,0:T(8,128)} %bias_hbm.1), custom_call_target="tpu_custom_call" | custom-call | flops 8000000000 | bytes 12000000 | tf_op jit(solution)/shard_map/pallas_call | solution.py:579
  142.0 2.8 %copy.8 = bf16[48,36,512]{2,0,1:T(8,128)(2,1)} copy(bf16[48,36,512]{2,0,1:T(8,128)(2,1)} %bitcast.4) | data formatting | bytes 3538944

commit v2 on v1

--- a/solution.py
+++ b/solution.py
@@ -87,6 +87,9 @@
     qk,
     vt,
     ctx,
+    head_mask,
+    place_in,
+    place_out,
     loc_sem,
     out_sem,
     z_send,
@@ -296,6 +299,15 @@
     lax.fori_loop(1, plane, send_pair, 0)
     sibling_pair_copy(core).start()
 
+    lane80 = lax.broadcasted_iota(I32, (80, 128), 1)
+    for k in range(4):
+        head_mask[k] = ((lane80 >= HD * k) & (lane80 < HD * k + HD)).astype(F32).astype(BF)
+    t_in = lax.broadcasted_iota(I32, (128, 192), 0)
+    place_in[...] = jnp.where(t_in < WIN, block_place(t_in), -1000)
+    t_out = lax.broadcasted_iota(I32, (192, 80), 1)
+    for k, (least, most) in enumerate(((0, WIN), (36, WIN), (0, 36))):
+        place_out[k] = jnp.where((t_out >= least) & (t_out < most), block_place(t_out), -1000)
+
     loads[4].wait()
     loads[5].wait()
     loads[6].wait()
@@ -306,7 +318,18 @@
         xn[c + 6, :, 0:C] = normed_rows(x, gain[...])
         return carry
 
-    lax.fori_loop(0, COLS, own_column, 0)
+    lax.fori_loop(0, COLS, own_column, 0, unroll=2)
+    set_out(1)
+
+    def pass_on(d, carry):
+        source = lax.rem(m + d, plane)
+        plane_copy(source * 2 + zhi, source, source, own_send.at[d], own_recv).wait_recv()
+        plane_copy(source * 2 + 1 - zhi, source, source, par_send.at[d], par_recv).wait_recv()
+        sibling_copy(core, source).start()
+        return carry
+
+    lax.fori_loop(1, plane // 2, pass_on, 0)
+    forward(0)
 
     def place_rows(count):
         half, c, r = token_parts(lax.broadcasted_iota(I32, (count, WIN), 0))
@@ -320,7 +343,10 @@
         bias[h] = dot_nt(keys_first, place_rows(128), lax.Precision.HIGHEST) * LOG2E
         return carry
 
-    lax.fori_loop(0, HEADS, bias_of, 0)
+    lax.fori_loop(0, HEADS, bias_of, 0, unroll=4)
+    lax.fori_loop(plane // 2, plane, pass_on, 0)
+    set_out(2)
+    forward(1)
     ctx[...] = jnp.zeros_like(ctx)
 
     for side in range(2):
@@ -341,38 +367,28 @@
         xn[e, :, C:WIDE] = (wide == code).astype(F32)
         return carry
 
-    lax.fori_loop(0, EXT, features, 0)
-    set_out(1)
-    forward(0)
+    lax.fori_loop(0, EXT, features, 0, unroll=4)
 
     def start_and_offset(i):
         start = 8 * ((13 * i) // 16)
         return start, 3 + 6 * i - start
 
-    def gather(i, j, u, w):
+    lane_in = lax.broadcasted_iota(I32, (128, 192), 1)
+
+    def gather_pair(i, first, second, u):
         start, offset = start_and_offset(i)
-        start = pl.multiple_of(start, 8)
-        block = xn[pl.ds(12 * j, 12), pl.ds(start, 16), :].reshape(192, WIDE).astype(BF)
-        t = lax.broadcasted_iota(I32, (128, 192), 0)
-        place = jnp.where(t < WIN, block_place(t), -1000) + offset
-        select = (lax.broadcasted_iota(I32, (128, 192), 1) == place).astype(F32).astype(BF)
-        xwin[u, 128 * w : 128 * w + 128, :] = dot(select, block).astype(BF)
+        if not isinstance(i, int):
+            start = pl.multiple_of(start, 8)
+        select = (lane_in - offset == place_in[...]).astype(F32).astype(BF)
+        for w, j in enumerate((first, second)):
+            block = xn[12 * j : 12 * j + 12, pl.ds(start, 16), :].reshape(192, WIDE).astype(BF)
+            xwin[u, 128 * w : 128 * w + 128, :] = dot(select, block).astype(BF)
 
     def gather_inner(i, carry):
-        gather(i, 1, i, 0)
-        gather(i, 2, i, 1)
+        gather_pair(i, 1, 2, i)
         return carry
 
     lax.fori_loop(0, 7, gather_inner, 0)
-
-    def pass_on(d, carry):
-        source = lax.rem(m + d, plane)
-        plane_copy(source * 2 + zhi, source, source, own_send.at[d], own_recv).wait_recv()
-        plane_copy(source * 2 + 1 - zhi, source, source, par_send.at[d], par_recv).wait_recv()
-        sibling_copy(core, source).start()
-        return carry
-
-    lax.fori_loop(1, plane, pass_on, 0)
 
     def await_sibling(d, carry):
         sibling_copy(1 - core, lax.rem(m + d, plane)).wait_recv()
@@ -380,8 +396,6 @@
 
     sibling_pair_copy(1 - core).wait_recv()
     lax.fori_loop(1, plane, await_sibling, 0)
-    set_out(2)
-    forward(1)
     eye_c = (
         lax.broadcasted_iota(I32, (C, C), 0) == lax.broadcasted_iota(I32, (C, C), 1)
     ).astype(F32).astype(BF)
@@ -457,7 +471,7 @@
                     [
                         jnp.concatenate(
                             [
-                                jnp.where(lane128 // HD == k, key, jnp.zeros_like(key)),
+                                key * head_mask[k],
                                 hot,
                             ],
                             axis=1,
@@ -478,7 +492,7 @@
         return dot(wpt[...], ctx[...]).astype(BF)
 
     def unit(u, carry):
-        @pl.when(u == 2)
+        @pl.when(u == 1)
         def _():
             forward(2)
 
@@ -488,8 +502,7 @@
             pk_top[144:288, :] = pack(0, 0)
             lat_copy(False).start()
             for n in range(2):
-                gather(n, 0, 7 + n, 0)
-                gather(n, 3, 7 + n, 1)
+                gather_pair(n, 0, 3, 7 + n)
 
         @pl.when(u == 9)
         def _():
@@ -497,8 +510,7 @@
             pk_bot[0:144, :] = pack(32, 13)
             lat_copy(True).start()
             for n in range(2):
-                gather(5 + n, 0, 9 + n, 0)
-                gather(5 + n, 3, 9 + n, 1)
+                gather_pair(5 + n, 0, 3, 9 + n)
 
         @pl.when(u == 11)
         def _():
@@ -510,8 +522,7 @@
         def _():
             halo_chunk(2)
             for n in range(3):
-                gather(2 + n, 0, 15 + n, 0)
-                gather(2 + n, 3, 15 + n, 1)
+                gather_pair(2 + n, 0, 3, 15 + n)
 
         att = attend(u)
         inner = u < 7
@@ -522,12 +533,10 @@
         start, offset = start_and_offset(i)
         start = jnp.where(edge, jnp.where(top, 0, 32), start)
         offset = jnp.where(edge, jnp.where(top, -3, 13), offset)
-        least = jnp.where(top, 36, 0)
-        most = jnp.where(bottom, 36, WIN)
+        kind = jnp.where(top, 1, jnp.where(bottom, 2, 0))
         start = pl.multiple_of(start, 8)
-        t = lax.broadcasted_iota(I32, (192, 80), 1)
-        place = jnp.where((t >= least) & (t < most), block_place(t) + offset, -1000)
-        select = (lax.broadcasted_iota(I32, (192, 80), 0) == place).astype(F32).astype(BF)
+        row = lax.broadcasted_iota(I32, (192, 80), 0)
+        select = (row - offset == place_out[kind]).astype(F32).astype(BF)
         for w in range(2):
             j = jnp.where(inner, 1 + w, jnp.where(edge, 2 * ((u - 11) % 2) + w, 3 * w))
             back = dot_nt(select, att[:, 128 * w : 128 * w + 80])
@@ -541,9 +550,13 @@
         xo[c] = acc[c + 6].astype(BF)
         return carry
 
-    lax.fori_loop(0, COLS, finish, 0)
-    store = pltpu.make_async_copy(xo, out, out_sem)
-    store.start()
+    def store(k):
+        part = pl.ds(9 * k, 9)
+        return pltpu.make_async_copy(xo.at[part], out.at[part], out_sem.at[k])
+
+    for k in range(4):
+        lax.fori_loop(9 * k, 9 * k + 9, finish, 0, unroll=3)
+        store(k).start()
 
     mirror_copy(lon).wait_send()
 
@@ -567,7 +580,8 @@
             halo_copy(side, k).wait_send()
     lat_copy(True).wait_send()
     lat_copy(False).wait_send()
-    store.wait()
+    for k in range(4):
+        store(k).wait()
 
 
 def local(tokens, region, ln_gain, qkv_weight, proj_weight, position_bias):
@@ -604,8 +618,11 @@
             vm((160, 1024), BF),
             vm((C, 256), BF),
             vm((C, 256), BF),
+            vm((4, 80, 128), BF),
+            vm((128, 192), I32),
+            vm((3, 192, 80), I32),
             dma((7,)),
-            dma,
+            dma((4,)),
             dma,
             dma,
             dma((plane,)),

time: 145 us -> 135 us (0.931)
  the two profiles are of different devices: /device:TPU:24 before, /device:TPU:38 now
where the time goes in v2:
time: 135 us
  Pallas kernels  132 us (98%)
  local copies, waits for them, and re-layouts  2.8 us (2%)
    pallas_call x1, Pallas kernels, local(): pl.pallas_call(functools.partial(kernel, nlat, nlon), out_shape=jax.Shape...  132 us
    unnamed x1, local copies, waits for them, and re-layouts  2.8 us

profile of v2, /device:TPU:38, one launch (start us, length us, event | category | flops | bytes accessed | tf_op | source)
XLA Modules:
  0.0 135.1 jit_solution(10489465169706522303)
XLA Ops:
  0.0 132.3 %shard_map.64 = bf16[36,48,512]{2,1,0:T(8,128)(2,1)} custom-call(bf16[36,48,512]{2,1,0:T(8,128)(2,1)} %bitcast.5, s32[36,48]{1,0:T(8,128)} %bitcast.6, f32[1,512]{1,0:T(1,128)} %bitcast.7, bf16[16,1536]{1,0:T(8,128)(2,1)} %wqkv.1, bf16[16,512]{1,0:T(8,128)(2,1)} %wproj.1, f32[16,72,72]{2,1,0:T(8,128)} %bias_hbm.1), custom_call_target="tpu_custom_call" | custom-call | flops 8000000000 | bytes 12000000 | tf_op jit(solution)/shard_map/pallas_call | solution.py:593
  132.3 2.8 %copy.8 = bf16[48,36,512]{2,0,1:T(8,128)(2,1)} copy(bf16[48,36,512]{2,0,1:T(8,128)(2,1)} %bitcast.4) | data formatting | bytes 3538944

commit v3 on v2

--- a/solution.py
+++ b/solution.py
@@ -26,6 +26,7 @@
 I32 = jnp.int32
 MESH = pl.DeviceIdType.MESH
 NT = (((1,), (1,)), ((), ()))
+TN = (((0,), (0,)), ((), ()))
 
 
 def dot(a, b):
@@ -77,15 +78,12 @@
     bias_raw,
     bias,
     wbuf,
-    wvt,
-    wpt,
     xn,
     acc,
     xwin,
     pk_top,
     pk_bot,
-    qk,
-    vt,
+    qkv,
     ctx,
     head_mask,
     place_in,
@@ -302,7 +300,7 @@
     lane80 = lax.broadcasted_iota(I32, (80, 128), 1)
     for k in range(4):
         head_mask[k] = ((lane80 >= HD * k) & (lane80 < HD * k + HD)).astype(F32).astype(BF)
-    t_in = lax.broadcasted_iota(I32, (128, 192), 0)
+    t_in = lax.broadcasted_iota(I32, (80, 192), 0)
     place_in[...] = jnp.where(t_in < WIN, block_place(t_in), -1000)
     t_out = lax.broadcasted_iota(I32, (192, 80), 1)
     for k, (least, most) in enumerate(((0, WIN), (36, WIN), (0, 36))):
@@ -338,16 +336,18 @@
         )
         return (lax.broadcasted_iota(I32, (count, WIN), 1) == place).astype(F32)
 
+    padded = lax.broadcasted_iota(I32, (80, 128), 0) >= WIN
+
     def bias_of(h, carry):
-        keys_first = dot_nt(place_rows(WIN), bias_raw[h], lax.Precision.HIGHEST)
-        bias[h] = dot_nt(keys_first, place_rows(128), lax.Precision.HIGHEST) * LOG2E
+        keys_first = dot_nt(place_rows(80), bias_raw[h], lax.Precision.HIGHEST)
+        placed = dot_nt(keys_first, place_rows(128), lax.Precision.HIGHEST)
+        bias[h] = jnp.where(padded, MASKED, placed * LOG2E)
         return carry
 
     lax.fori_loop(0, HEADS, bias_of, 0, unroll=4)
     lax.fori_loop(plane // 2, plane, pass_on, 0)
     set_out(2)
     forward(1)
-    ctx[...] = jnp.zeros_like(ctx)
 
     for side in range(2):
         label_copy(side).wait_recv()
@@ -373,7 +373,7 @@
         start = 8 * ((13 * i) // 16)
         return start, 3 + 6 * i - start
 
-    lane_in = lax.broadcasted_iota(I32, (128, 192), 1)
+    lane_in = lax.broadcasted_iota(I32, (80, 192), 1)
 
     def gather_pair(i, first, second, u):
         start, offset = start_and_offset(i)
@@ -382,7 +382,7 @@
         select = (lane_in - offset == place_in[...]).astype(F32).astype(BF)
         for w, j in enumerate((first, second)):
             block = xn[12 * j : 12 * j + 12, pl.ds(start, 16), :].reshape(192, WIDE).astype(BF)
-            xwin[u, 128 * w : 128 * w + 128, :] = dot(select, block).astype(BF)
+            xwin[u, 80 * w : 80 * w + 80, :] = dot(select, block).astype(BF)
 
     def gather_inner(i, carry):
         gather_pair(i, 1, 2, i)
@@ -396,12 +396,6 @@
 
     sibling_pair_copy(1 - core).wait_recv()
     lax.fori_loop(1, plane, await_sibling, 0)
-    eye_c = (
-        lax.broadcasted_iota(I32, (C, C), 0) == lax.broadcasted_iota(I32, (C, C), 1)
-    ).astype(F32).astype(BF)
-    wvt[...] = dot_nt(eye_c, wbuf[1, :, 0:512]).astype(BF)
-    wpt[...] = dot_nt(eye_c, wbuf[1, :, 512:1024]).astype(BF)
-
     def halo_chunk(k):
         row = (0, 32, 16)[k]
         for side in range(2):
@@ -443,53 +437,50 @@
         )
 
     def gather_edges():
-        t = lax.broadcasted_iota(I32, (128, 288), 0)
-        lane = lax.broadcasted_iota(I32, (128, 288), 1)
+        t = lax.broadcasted_iota(I32, (80, 288), 0)
+        lane = lax.broadcasted_iota(I32, (80, 288), 1)
         place = jnp.where(t < WIN, t + 108 * (t >= 36).astype(I32), -1000)
         for j in range(4):
             select = (lane == place + 36 * j).astype(F32).astype(BF)
             for k, rows in enumerate((pk_top, pk_bot)):
-                xwin[11 + 2 * k + j // 2, 128 * (j % 2) : 128 * (j % 2) + 128, :] = dot(
+                xwin[11 + 2 * k + j // 2, 80 * (j % 2) : 80 * (j % 2) + 80, :] = dot(
                     select, rows[...]
                 ).astype(BF)
 
     lane128 = lax.broadcasted_iota(I32, (80, 128), 1)
 
     def attend(u):
-        first = xwin[u, 0:80, :]
-        second = xwin[u, 128:208, :]
-        both = jnp.concatenate([first[:, 0:C], second[:, 0:C]], axis=0)
-        qk[...] = dot(both, wbuf[0]).astype(BF)
-        vt[...] = dot_nt(wvt[...], xwin[u, :, 0:C]).astype(BF)
+        both = xwin[u, :, 0:C]
+        qkv[:, 0:1024] = dot(both, wbuf[0]).astype(BF)
+        qkv[:, 1024:1536] = dot(both, wbuf[1, :, 0:C]).astype(BF)
         for w in range(2):
-            hot = (first, second)[w][:, C:WIDE]
+            rows = slice(80 * w, 80 * w + 80)
+            hot = xwin[u, rows, C:WIDE]
             differs = jnp.where(lane128 < 6, MASKED * (1.0 - hot.astype(F32)), 0.0).astype(BF)
             for g in range(4):
-                query = qk[80 * w : 80 * w + 80, 128 * g : 128 * g + 128]
-                key = qk[80 * w : 80 * w + 80, 512 + 128 * g : 640 + 128 * g]
-                stacked = jnp.concatenate(
+                query, key, value = (
+                    qkv[rows, C * part + 128 * g : C * part + 128 * g + 128] for part in range(3)
+                )
+                keys = jnp.concatenate(
+                    [jnp.concatenate([key * head_mask[k], hot], axis=1) for k in range(4)], axis=0
+                )
+                scores = dot_nt(keys, jnp.concatenate([query, differs], axis=1))
+                s = scores.reshape(4, 80, 80) * SCALE + bias[4 * g : 4 * g + 4, :, 0:80]
+                e = jnp.exp2(s - jnp.max(s, axis=1, keepdims=True))
+                values = jnp.concatenate(
                     [
-                        jnp.concatenate(
-                            [
-                                key * head_mask[k],
-                                hot,
-                            ],
-                            axis=1,
-                        )
+                        jnp.concatenate([value * head_mask[k], head_mask[k]], axis=1)
                         for k in range(4)
                     ],
                     axis=0,
                 )
-                scores = dot_nt(stacked, jnp.concatenate([query, differs], axis=1))
-                for k in range(4):
-                    h = 4 * g + k
-                    s = scores[80 * k : 80 * k + WIN] * SCALE + bias[h, :, 0:80]
-                    e = jnp.exp2(s - jnp.max(s, axis=0, keepdims=True))
-                    total = jnp.sum(e, axis=0, keepdims=True)
-                    probs = jnp.concatenate([e, jnp.zeros((8, 80), F32)], axis=0).astype(BF)
-                    part = dot(vt[HD * h : HD * h + HD, 128 * w : 128 * w + 80], probs)
-                    ctx[HD * h : HD * h + HD, 128 * w : 128 * w + 80] = (part * (1.0 / total)).astype(BF)
-        return dot(wpt[...], ctx[...]).astype(BF)
+                summed = lax.dot_general(
+                    e.reshape(320, 80).astype(BF), values, TN, preferred_element_type=F32
+                )
+                ctx[rows, 128 * g : 128 * g + 128] = (
+                    summed[:, 0:128] * (1.0 / summed[:, 128:256])
+                ).astype(BF)
+        return dot(ctx[...], wbuf[1, :, 512:1024]).astype(BF)
 
     def unit(u, carry):
         @pl.when(u == 1)
@@ -539,7 +530,7 @@
         select = (row - offset == place_out[kind]).astype(F32).astype(BF)
         for w in range(2):
             j = jnp.where(inner, 1 + w, jnp.where(edge, 2 * ((u - 11) % 2) + w, 3 * w))
-            back = dot_nt(select, att[:, 128 * w : 128 * w + 80])
+            back = dot(select, att[80 * w : 80 * w + 80])
             spot = (pl.ds(12 * j, 12), pl.ds(start, 16), slice(None))
             acc[spot] = acc[spot] + back.reshape(12, 16, C)
         return carry
@@ -606,20 +597,17 @@
             vm((ROWS, EXT), F32),
             vm((1, C), F32),
             vm((HEADS, WIN, WIN), F32),
-            vm((HEADS, WIN, 128), F32),
+            vm((HEADS, 80, 128), F32),
             vm((2, C, 1024), BF),
-            vm((C, C), BF),
-            vm((C, C), BF),
             vm((EXT, ROWS, WIDE), F32),
             vm((EXT, ROWS, C), F32),
-            vm((UNITS, 256, WIDE), BF),
+            vm((UNITS, 160, WIDE), BF),
             vm((288, WIDE), BF),
             vm((288, WIDE), BF),
-            vm((160, 1024), BF),
-            vm((C, 256), BF),
-            vm((C, 256), BF),
+            vm((160, 3 * C), BF),
+            vm((160, C), BF),
             vm((4, 80, 128), BF),
-            vm((128, 192), I32),
+            vm((80, 192), I32),
             vm((3, 192, 80), I32),
             dma((7,)),
             dma((4,)),

time: 135 us -> 133 us (0.985)
  the two profiles are of different devices: /device:TPU:38 before, /device:TPU:34 now
where the time goes in v3:
time: 133 us
  Pallas kernels  130 us (98%)
  local copies, waits for them, and re-layouts  2.8 us (2%)
    pallas_call x1, Pallas kernels, local(): pl.pallas_call(functools.partial(kernel, nlat, nlon), out_shape=jax.Shape...  130 us
    unnamed x1, local copies, waits for them, and re-layouts  2.8 us

profile of v3, /device:TPU:34, one launch (start us, length us, event | category | flops | bytes accessed | tf_op | source)
XLA Modules:
  0.0 133.0 jit_solution(5187812320646622638)
XLA Ops:
  0.0 130.2 %shard_map.64 = bf16[36,48,512]{2,1,0:T(8,128)(2,1)} custom-call(bf16[36,48,512]{2,1,0:T(8,128)(2,1)} %bitcast.5, s32[36,48]{1,0:T(8,128)} %bitcast.6, f32[1,512]{1,0:T(1,128)} %bitcast.7, bf16[16,1536]{1,0:T(8,128)(2,1)} %wqkv.1, bf16[16,512]{1,0:T(8,128)(2,1)} %wproj.1, f32[16,72,72]{2,1,0:T(8,128)} %bias_hbm.1), custom_call_target="tpu_custom_call" | custom-call | flops 8000000000 | bytes 12000000 | tf_op jit(solution)/shard_map/pallas_call | solution.py:584
  130.2 2.8 %copy.8 = bf16[48,36,512]{2,0,1:T(8,128)(2,1)} copy(bf16[48,36,512]{2,0,1:T(8,128)(2,1)} %bitcast.4) | data formatting | bytes 3538944

commit v4 on v3

--- a/solution.py
+++ b/solution.py
@@ -92,10 +92,10 @@
     out_sem,
     z_send,
     z_recv,
-    own_send,
-    own_recv,
-    par_send,
-    par_recv,
+    line_send,
+    line_recv,
+    block_send,
+    block_recv,
     sib_send,
     sib_recv,
     leg_send,
@@ -121,6 +121,9 @@
     lon_pair = lon + 1 - 2 * zhi
     lat_mirror = (nlat // 2 - 1 - lat // 2) * 2 + core
     lat_sib = lat + 1 - 2 * core
+    nx = min(4, plane)
+    ny = plane // nx
+    y, x = m // nx, lax.rem(m, nx)
 
     zlo = nlat // 2
     ring = 2 * zlo
@@ -144,16 +147,27 @@
         chip_at(lon_up // 2, lax.rem(lon_up, 2) * zlo + lat // 2 - leg),
     )
 
+    own_rows = pl.ds(zhi * shard, shard)
+
+    def quarter_load(k, source):
+        return pltpu.make_async_copy(source, wbuf.at[k, y, x, own_rows, :], loc_sem.at[k % 2])
+
+    quarters = (
+        (quarter_load(0, wqkv.at[:, 0:C]), quarter_load(1, wqkv.at[:, C : 2 * C])),
+        (quarter_load(2, wqkv.at[:, 2 * C : 3 * C]), quarter_load(3, wproj)),
+    )
+    for c in range(2):
+
+        @pl.when(core == c)
+        def _():
+            for copy in quarters[c]:
+                copy.start()
+
     loads = [
-        pltpu.make_async_copy(wqkv.at[:, 0:1024], wbuf.at[0, pl.ds(lon * shard, shard), :], loc_sem.at[0]),
-        pltpu.make_async_copy(
-            wqkv.at[:, 1024:1536], wbuf.at[1, pl.ds(lon * shard, shard), 0:512], loc_sem.at[1]
-        ),
-        pltpu.make_async_copy(wproj, wbuf.at[1, pl.ds(lon * shard, shard), 512:1024], loc_sem.at[2]),
-        pltpu.make_async_copy(reg, lab_own, loc_sem.at[3]),
-        pltpu.make_async_copy(tok, xo, loc_sem.at[4]),
-        pltpu.make_async_copy(gain_hbm, gain, loc_sem.at[5]),
-        pltpu.make_async_copy(bias_hbm, bias_raw, loc_sem.at[6]),
+        pltpu.make_async_copy(reg, lab_own, loc_sem.at[2]),
+        pltpu.make_async_copy(tok, xo, loc_sem.at[3]),
+        pltpu.make_async_copy(gain_hbm, gain, loc_sem.at[4]),
+        pltpu.make_async_copy(bias_hbm, bias_raw, loc_sem.at[5]),
     ]
     for copy in loads:
         copy.start()
@@ -169,74 +183,101 @@
         below,
     )
     greeted = greeted + relays_here
+    greeted = greeted + tuple((lat, (y * nx + lax.rem(x + d, nx)) * 2 + zhi) for d in range(1, nx))
+    greeted = greeted + tuple((lat, (lax.rem(y + d, ny) * nx + x) * 2 + zhi) for d in range(1, ny))
     for there in greeted:
         pl.semaphore_signal(barrier, inc=1, device_id=there, device_id_type=MESH)
-
-    def greet(d, carry):
-        pl.semaphore_signal(
-            barrier,
-            inc=1,
-            device_id=(lat, lax.rem(m + d, plane) * 2 + zhi),
-            device_id_type=MESH,
-        )
-        return carry
-
-    lax.fori_loop(1, plane, greet, 0)
-    pl.semaphore_wait(barrier, len(greeted) + plane - 1)
-
-    def mirror_copy(rows_of):
-        rows = pl.ds(rows_of * shard, shard)
-        return pltpu.make_async_remote_copy(
-            src_ref=wbuf.at[core, rows, :],
-            dst_ref=wbuf.at[core, rows, :],
+    pl.semaphore_wait(barrier, len(greeted))
+
+    def plane_device(py, px):
+        return lat, (py * nx + px) * 2 + zhi
+
+    def at_x(d):
+        return lax.rem(x + d, nx)
+
+    def at_y(d):
+        return lax.rem(y + d, ny)
+
+    def mirror_copy(of):
+        part = wbuf.at[pl.ds(2 * core, 2), y, x, pl.ds(of * shard, shard), :]
+        return pltpu.make_async_remote_copy(
+            src_ref=part,
+            dst_ref=part,
             send_sem=z_send,
             recv_sem=z_recv,
             device_id=(lat_mirror, lon_pair),
             device_id_type=MESH,
         )
 
-    def plane_copy(rows_of, other, mark, send, recv):
-        rows = pl.ds(rows_of * shard, shard)
-        return pltpu.make_async_remote_copy(
-            src_ref=wbuf.at[core, rows, :],
-            dst_ref=wbuf.at[core, rows, :],
-            send_sem=send,
-            recv_sem=recv.at[mark],
-            device_id=(lat, other * 2 + zhi),
-            device_id_type=MESH,
-        )
-
-    def sibling_copy(half, owner):
-        rows = pl.ds(owner * 2 * shard, 2 * shard)
-        return pltpu.make_async_remote_copy(
-            src_ref=wbuf.at[half, rows, :],
-            dst_ref=wbuf.at[half, rows, :],
-            send_sem=sib_send.at[owner],
-            recv_sem=sib_recv.at[owner],
+    def line_copy(a, d, owner):
+        py, px = (y, owner) if a == 0 else (owner, x)
+        part = wbuf.at[2 * core + a, py, px]
+        return pltpu.make_async_remote_copy(
+            src_ref=part,
+            dst_ref=part,
+            send_sem=line_send.at[a, d],
+            recv_sem=line_recv.at[a, owner],
+            device_id=plane_device(y, at_x(d)) if a == 0 else plane_device(at_y(d), x),
+            device_id_type=MESH,
+        )
+
+    def block_of(half, a, owner):
+        return wbuf.at[2 * half, owner] if a == 0 else wbuf.at[2 * half + 1, :, owner]
+
+    def block_copy(a, d, owner):
+        part = block_of(core, a, owner)
+        return pltpu.make_async_remote_copy(
+            src_ref=part,
+            dst_ref=part,
+            send_sem=block_send.at[a, d],
+            recv_sem=block_recv.at[a, owner],
+            device_id=plane_device(at_y(d), x) if a == 0 else plane_device(y, at_x(d)),
+            device_id_type=MESH,
+        )
+
+    def sibling_copy(half, a, owner):
+        part = block_of(half, a, owner)
+        return pltpu.make_async_remote_copy(
+            src_ref=part,
+            dst_ref=part,
+            send_sem=sib_send.at[a, owner],
+            recv_sem=sib_recv.at[a, owner],
             device_id=(lat_sib, lon),
             device_id_type=MESH,
         )
 
-    def sibling_pair_copy(half):
-        rows = pl.ds(lon_pair * shard, shard)
-        return pltpu.make_async_remote_copy(
-            src_ref=wbuf.at[half, rows, :],
-            dst_ref=wbuf.at[half, rows, :],
-            send_sem=sib_send.at[m],
-            recv_sem=sib_recv.at[m],
-            device_id=(lat_sib, lon),
-            device_id_type=MESH,
-        )
-
-    for k in range(3):
-        loads[k].wait()
-    mirror_copy(lon).start()
-
-    def send_own(d, carry):
-        plane_copy(lon, lax.rem(m + d, plane), m, own_send.at[d], own_recv).start()
-        return carry
-
-    lax.fori_loop(1, plane, send_own, 0)
+    first_axis = ((nx, x, at_x), (ny, y, at_y))
+    second_axis = ((ny, y, at_y), (nx, x, at_x))
+
+    def send_lines():
+        for a, (n, me, _) in enumerate(first_axis):
+            for d in range(1, n):
+                line_copy(a, d, me).start()
+
+    def send_blocks():
+        for a, (n, _, at) in enumerate(first_axis):
+            for d in range(1, n):
+                line_copy(a, d, at(d)).wait_recv()
+        for a, (n, me, _) in enumerate(second_axis):
+            for d in range(1, n):
+                block_copy(a, d, me).start()
+            sibling_copy(core, a, me).start()
+
+    def pass_on():
+        for d in range(1, max(nx, ny)):
+            for a, (n, _, at) in enumerate(second_axis):
+                if d < n:
+                    block_copy(a, d, at(d)).wait_recv()
+                    sibling_copy(core, a, at(d)).start()
+
+    for c in range(2):
+
+        @pl.when(core == c)
+        def _():
+            for copy in quarters[c]:
+                copy.wait()
+
+    mirror_copy(zhi).start()
 
     def leg_copy(side, k):
         rows = pl.ds((0, 32, 16)[k], 16)
@@ -280,7 +321,7 @@
             device_id_type=MESH,
         )
 
-    loads[3].wait()
+    loads[0].wait()
     lab_send[...] = jnp.zeros_like(lab_send)
     lab_send[0, 0:6, 0:ROWS] = lab_own[COLS - 6 : COLS, :]
     lab_send[1, 0:6, 0:ROWS] = lab_own[0:6, :]
@@ -288,14 +329,9 @@
         label_copy(side).start()
     set_out(0)
 
-    mirror_copy(lon_pair).wait_recv()
-
-    def send_pair(d, carry):
-        plane_copy(lon_pair, lax.rem(m + d, plane), m, par_send.at[d], par_recv).start()
-        return carry
-
-    lax.fori_loop(1, plane, send_pair, 0)
-    sibling_pair_copy(core).start()
+    mirror_copy(1 - zhi).wait_recv()
+    send_lines()
+    set_out(1)
 
     lane80 = lax.broadcasted_iota(I32, (80, 128), 1)
     for k in range(4):
@@ -306,9 +342,9 @@
     for k, (least, most) in enumerate(((0, WIN), (36, WIN), (0, 36))):
         place_out[k] = jnp.where((t_out >= least) & (t_out < most), block_place(t_out), -1000)
 
-    loads[4].wait()
-    loads[5].wait()
-    loads[6].wait()
+    loads[1].wait()
+    loads[2].wait()
+    loads[3].wait()
 
     def own_column(c, carry):
         x = xo[c].astype(F32)
@@ -317,17 +353,9 @@
         return carry
 
     lax.fori_loop(0, COLS, own_column, 0, unroll=2)
-    set_out(1)
-
-    def pass_on(d, carry):
-        source = lax.rem(m + d, plane)
-        plane_copy(source * 2 + zhi, source, source, own_send.at[d], own_recv).wait_recv()
-        plane_copy(source * 2 + 1 - zhi, source, source, par_send.at[d], par_recv).wait_recv()
-        sibling_copy(core, source).start()
-        return carry
-
-    lax.fori_loop(1, plane // 2, pass_on, 0)
+    send_blocks()
     forward(0)
+    set_out(2)
 
     def place_rows(count):
         half, c, r = token_parts(lax.broadcasted_iota(I32, (count, WIN), 0))
@@ -345,9 +373,9 @@
         return carry
 
     lax.fori_loop(0, HEADS, bias_of, 0, unroll=4)
-    lax.fori_loop(plane // 2, plane, pass_on, 0)
-    set_out(2)
     forward(1)
+    pass_on()
+    forward(2)
 
     for side in range(2):
         label_copy(side).wait_recv()
@@ -390,12 +418,10 @@
 
     lax.fori_loop(0, 7, gather_inner, 0)
 
-    def await_sibling(d, carry):
-        sibling_copy(1 - core, lax.rem(m + d, plane)).wait_recv()
-        return carry
-
-    sibling_pair_copy(1 - core).wait_recv()
-    lax.fori_loop(1, plane, await_sibling, 0)
+    for a, (n, _, at) in enumerate(second_axis):
+        for d in range(n):
+            sibling_copy(1 - core, a, at(d)).wait_recv()
+
     def halo_chunk(k):
         row = (0, 32, 16)[k]
         for side in range(2):
@@ -449,10 +475,13 @@
 
     lane128 = lax.broadcasted_iota(I32, (80, 128), 1)
 
+    def weight(k):
+        return wbuf[k].reshape(C, C)
+
     def attend(u):
         both = xwin[u, :, 0:C]
-        qkv[:, 0:1024] = dot(both, wbuf[0]).astype(BF)
-        qkv[:, 1024:1536] = dot(both, wbuf[1, :, 0:C]).astype(BF)
+        for part in range(3):
+            qkv[:, C * part : C * part + C] = dot(both, weight(part)).astype(BF)
         for w in range(2):
             rows = slice(80 * w, 80 * w + 80)
             hot = xwin[u, rows, C:WIDE]
@@ -480,13 +509,9 @@
                 ctx[rows, 128 * g : 128 * g + 128] = (
                     summed[:, 0:128] * (1.0 / summed[:, 128:256])
                 ).astype(BF)
-        return dot(ctx[...], wbuf[1, :, 512:1024]).astype(BF)
+        return dot(ctx[...], weight(3)).astype(BF)
 
     def unit(u, carry):
-        @pl.when(u == 1)
-        def _():
-            forward(2)
-
         @pl.when(u == 7)
         def _():
             halo_chunk(0)
@@ -549,21 +574,15 @@
         lax.fori_loop(9 * k, 9 * k + 9, finish, 0, unroll=3)
         store(k).start()
 
-    mirror_copy(lon).wait_send()
-
-    def sent(d, carry):
-        plane_copy(lon, lax.rem(m + d, plane), m, own_send.at[d], own_recv).wait_send()
-        plane_copy(lon_pair, lax.rem(m + d, plane), m, par_send.at[d], par_recv).wait_send()
-        return carry
-
-    lax.fori_loop(1, plane, sent, 0)
-
-    def sent_on(d, carry):
-        sibling_copy(core, lax.rem(m + d, plane)).wait_send()
-        return carry
-
-    sibling_pair_copy(core).wait_send()
-    lax.fori_loop(1, plane, sent_on, 0)
+    mirror_copy(zhi).wait_send()
+    for a, (n, me, _) in enumerate(first_axis):
+        for d in range(1, n):
+            line_copy(a, d, me).wait_send()
+    for a, (n, me, at) in enumerate(second_axis):
+        for d in range(1, n):
+            block_copy(a, d, me).wait_send()
+        for d in range(n):
+            sibling_copy(core, a, at(d)).wait_send()
     for side in range(2):
         label_copy(side).wait_send()
         for k in range(3):
@@ -579,6 +598,8 @@
     nlat = lax.axis_size("lat")
     nlon = lax.axis_size("lon")
     plane = nlon // 2
+    nx = min(4, plane)
+    ny = plane // nx
     dma = pltpu.SemaphoreType.DMA
     vm = pltpu.VMEM
     mixed = pl.pallas_call(
@@ -598,7 +619,7 @@
             vm((1, C), F32),
             vm((HEADS, WIN, WIN), F32),
             vm((HEADS, 80, 128), F32),
-            vm((2, C, 1024), BF),
+            vm((4, ny, nx, 2 * (C // nlon), C), BF),
             vm((EXT, ROWS, WIDE), F32),
             vm((EXT, ROWS, C), F32),
             vm((UNITS, 160, WIDE), BF),
@@ -609,16 +630,16 @@
             vm((4, 80, 128), BF),
             vm((80, 192), I32),
             vm((3, 192, 80), I32),
-            dma((7,)),
+            dma((6,)),
             dma((4,)),
             dma,
             dma,
-            dma((plane,)),
-            dma((plane,)),
-            dma((plane,)),
-            dma((plane,)),
-            dma((plane,)),
-            dma((plane,)),
+            dma((2, nx)),
+            dma((2, nx)),
+            dma((2, nx)),
+            dma((2, nx)),
+            dma((2, nx)),
+            dma((2, nx)),
             dma((2, 3)),
             dma((2, 3)),
             dma((2, 3)),

time: 133 us -> 137 us (1.030)
  the two profiles are of different devices: /device:TPU:34 before, /device:TPU:72 now
where the time goes in v4:
time: 137 us
  Pallas kernels  134 us (98%)
  local copies, waits for them, and re-layouts  2.8 us (2%)
    pallas_call x1, Pallas kernels, local(): pl.pallas_call(functools.partial(kernel, nlat, nlon), out_shape=jax.Shape...  134 us
    unnamed x1, local copies, waits for them, and re-layouts  2.8 us

profile of v4, /device:TPU:72, one launch (start us, length us, event | category | flops | bytes accessed | tf_op | source)
XLA Modules:
  0.0 136.9 jit_solution(17253286672153817307)
XLA Ops:
  0.0 134.1 %shard_map.64 = bf16[36,48,512]{2,1,0:T(8,128)(2,1)} custom-call(bf16[36,48,512]{2,1,0:T(8,128)(2,1)} %bitcast.5, s32[36,48]{1,0:T(8,128)} %bitcast.6, f32[1,512]{1,0:T(1,128)} %bitcast.7, bf16[16,1536]{1,0:T(8,128)(2,1)} %wqkv.1, bf16[16,512]{1,0:T(8,128)(2,1)} %wproj.1, f32[16,72,72]{2,1,0:T(8,128)} %bias_hbm.1), custom_call_target="tpu_custom_call" | custom-call | flops 8000000000 | bytes 12000000 | tf_op jit(solution)/shard_map/pallas_call | solution.py:605
  134.1 2.8 %copy.8 = bf16[48,36,512]{2,0,1:T(8,128)(2,1)} copy(bf16[48,36,512]{2,0,1:T(8,128)(2,1)} %bitcast.4) | data formatting | bytes 3538944

commit v5 on v4

--- a/solution.py
+++ b/solution.py
@@ -88,6 +88,7 @@
     head_mask,
     place_in,
     place_out,
+    second_owns,
     loc_sem,
     out_sem,
     z_send,
@@ -329,16 +330,16 @@
         label_copy(side).start()
     set_out(0)
 
-    mirror_copy(1 - zhi).wait_recv()
-    send_lines()
-    set_out(1)
-
     lane80 = lax.broadcasted_iota(I32, (80, 128), 1)
     for k in range(4):
         head_mask[k] = ((lane80 >= HD * k) & (lane80 < HD * k + HD)).astype(F32).astype(BF)
     t_in = lax.broadcasted_iota(I32, (80, 192), 0)
     place_in[...] = jnp.where(t_in < WIN, block_place(t_in), -1000)
     t_out = lax.broadcasted_iota(I32, (192, 80), 1)
+    t_row = lax.broadcasted_iota(I32, (80, 128), 0)
+    within = t_row - 36 * (t_row >= 36).astype(I32)
+    second_owns[0] = (within < 18).astype(F32)
+    second_owns[1] = (t_row < 36).astype(F32)
     for k, (least, most) in enumerate(((0, WIN), (36, WIN), (0, 36))):
         place_out[k] = jnp.where((t_out >= least) & (t_out < most), block_place(t_out), -1000)
 
@@ -352,7 +353,11 @@
         xn[c + 6, :, 0:C] = normed_rows(x, gain[...])
         return carry
 
-    lax.fori_loop(0, COLS, own_column, 0, unroll=2)
+    lax.fori_loop(0, COLS // 2, own_column, 0, unroll=2)
+    mirror_copy(1 - zhi).wait_recv()
+    send_lines()
+    set_out(1)
+    lax.fori_loop(COLS // 2, COLS, own_column, 0, unroll=2)
     send_blocks()
     forward(0)
     set_out(2)
@@ -469,7 +474,7 @@
         for j in range(4):
             select = (lane == place + 36 * j).astype(F32).astype(BF)
             for k, rows in enumerate((pk_top, pk_bot)):
-                xwin[11 + 2 * k + j // 2, 80 * (j % 2) : 80 * (j % 2) + 80, :] = dot(
+                xwin[11 + j, 80 * k : 80 * k + 80, :] = dot(
                     select, rows[...]
                 ).astype(BF)
 
@@ -478,41 +483,98 @@
     def weight(k):
         return wbuf[k].reshape(C, C)
 
-    def attend(u):
+    def project(u):
         both = xwin[u, :, 0:C]
         for part in range(3):
             qkv[:, C * part : C * part + C] = dot(both, weight(part)).astype(BF)
+
+    def mask_features(u, w):
+        hot = xwin[u, 80 * w : 80 * w + 80, C:WIDE]
+        differs = jnp.where(lane128 < 6, MASKED * (1.0 - hot.astype(F32)), 0.0).astype(BF)
+        return hot, differs
+
+    def parts_of(w, g):
+        rows = slice(80 * w, 80 * w + 80)
+        return (qkv[rows, C * part + 128 * g : C * part + 128 * g + 128] for part in range(3))
+
+    def stack(pieces):
+        return jnp.concatenate(
+            [jnp.concatenate(pieces(head_mask[k]), axis=1) for k in range(4)], axis=0
+        )
+
+    def weights_of(scores, g):
+        s = scores.reshape(4, 80, 80) * SCALE + bias[4 * g : 4 * g + 4, :, 0:80]
+        e = jnp.exp2(s - jnp.max(s, axis=1, keepdims=True))
+        return e.reshape(320, 80).astype(BF)
+
+    def over_keys(e, values):
+        return lax.dot_general(e, values, TN, preferred_element_type=F32)
+
+    def attend_two(u):
+        project(u)
         for w in range(2):
-            rows = slice(80 * w, 80 * w + 80)
-            hot = xwin[u, rows, C:WIDE]
-            differs = jnp.where(lane128 < 6, MASKED * (1.0 - hot.astype(F32)), 0.0).astype(BF)
+            hot, differs = mask_features(u, w)
             for g in range(4):
-                query, key, value = (
-                    qkv[rows, C * part + 128 * g : C * part + 128 * g + 128] for part in range(3)
+                query, key, value = parts_of(w, g)
+                scores = dot_nt(
+                    stack(lambda mask: [key * mask, hot]),
+                    jnp.concatenate([query, differs], axis=1),
                 )
-                keys = jnp.concatenate(
-                    [jnp.concatenate([key * head_mask[k], hot], axis=1) for k in range(4)], axis=0
-                )
-                scores = dot_nt(keys, jnp.concatenate([query, differs], axis=1))
-                s = scores.reshape(4, 80, 80) * SCALE + bias[4 * g : 4 * g + 4, :, 0:80]
-                e = jnp.exp2(s - jnp.max(s, axis=1, keepdims=True))
-                values = jnp.concatenate(
-                    [
-                        jnp.concatenate([value * head_mask[k], head_mask[k]], axis=1)
-                        for k in range(4)
-                    ],
-                    axis=0,
-                )
-                summed = lax.dot_general(
-                    e.reshape(320, 80).astype(BF), values, TN, preferred_element_type=F32
-                )
-                ctx[rows, 128 * g : 128 * g + 128] = (
+                summed = over_keys(weights_of(scores, g), stack(lambda mask: [value * mask, mask]))
+                ctx[80 * w : 80 * w + 80, 128 * g : 128 * g + 128] = (
                     summed[:, 0:128] * (1.0 / summed[:, 128:256])
                 ).astype(BF)
         return dot(ctx[...], weight(3)).astype(BF)
 
-    def unit(u, carry):
-        @pl.when(u == 7)
+    def attend_merged(u, kind):
+        project(u)
+        of_second = second_owns[kind]
+        keep1 = of_second.astype(BF)
+        keep0 = (1.0 - of_second).astype(BF)
+        hot0, differs0 = mask_features(u, 0)
+        hot1, differs1 = mask_features(u, 1)
+        differs0 = differs0 * keep0
+        differs1 = differs1 * keep1
+        for g in range(4):
+            query0, key0, value0 = parts_of(0, g)
+            query1, key1, value1 = parts_of(1, g)
+            scores = dot_nt(
+                stack(lambda mask: [key0 * mask, hot0, key1 * mask, hot1]),
+                jnp.concatenate([query0 * keep0, differs0, query1 * keep1, differs1], axis=1),
+            )
+            summed = over_keys(
+                weights_of(scores, g), stack(lambda mask: [value0 * mask, value1 * mask, mask])
+            )
+            own = jnp.where(of_second > 0.5, summed[:, 128:256], summed[:, 0:128])
+            ctx[0:80, 128 * g : 128 * g + 128] = (own * (1.0 / summed[:, 256:384])).astype(BF)
+        return dot(ctx[0:80, :], weight(3)).astype(BF)
+
+    row_out = lax.broadcasted_iota(I32, (192, 80), 0)
+
+    def add_back(att, j, start, offset, kind):
+        select = (row_out - offset == place_out[kind]).astype(F32).astype(BF)
+        spot = (pl.ds(12 * j, 12), pl.ds(pl.multiple_of(start, 8), 16), slice(None))
+        acc[spot] = acc[spot] + dot(select, att).reshape(12, 16, C)
+
+    def inner_unit(u, carry):
+        att = attend_two(u)
+        start, offset = start_and_offset(u)
+        for w in range(2):
+            add_back(att[80 * w : 80 * w + 80], 1 + w, start, offset, 0)
+        return carry
+
+    lax.fori_loop(0, 7, inner_unit, 0)
+
+    def finish(c, carry):
+        xo[c] = acc[c + 6].astype(BF)
+        return carry
+
+    def store(k):
+        part = (pl.ds(0, 6), pl.ds(6, COLS - 12), pl.ds(COLS - 6, 6))[k]
+        return pltpu.make_async_copy(xo.at[part], out.at[part], out_sem.at[k])
+
+    def merged_unit(v, carry):
+        @pl.when(v == 0)
         def _():
             halo_chunk(0)
             pk_top[144:288, :] = pack(0, 0)
@@ -520,7 +582,7 @@
             for n in range(2):
                 gather_pair(n, 0, 3, 7 + n)
 
-        @pl.when(u == 9)
+        @pl.when(v == 2)
         def _():
             halo_chunk(1)
             pk_bot[0:144, :] = pack(32, 13)
@@ -528,50 +590,38 @@
             for n in range(2):
                 gather_pair(5 + n, 0, 3, 9 + n)
 
-        @pl.when(u == 11)
+        @pl.when(v == 4)
         def _():
             lat_copy(True).wait_recv()
             lat_copy(False).wait_recv()
             gather_edges()
 
-        @pl.when(u == 15)
+        @pl.when(v == 8)
         def _():
+            lax.fori_loop(6, COLS - 6, finish, 0, unroll=3)
+            store(1).start()
             halo_chunk(2)
             for n in range(3):
                 gather_pair(2 + n, 0, 3, 15 + n)
 
-        att = attend(u)
-        inner = u < 7
-        edge = (u >= 11) & (u < 15)
-        top = edge & (u < 13)
-        bottom = edge & (u >= 13)
-        i = jnp.where(inner, u, jnp.where(u < 9, u - 7, jnp.where(u < 11, u - 4, u - 13)))
+        edge = ((v >= 4) & (v < 8)).astype(I32)
+        att = attend_merged(7 + v, edge)
+        i = jnp.where(v < 2, v, jnp.where(v < 4, v + 3, v - 6))
         start, offset = start_and_offset(i)
-        start = jnp.where(edge, jnp.where(top, 0, 32), start)
-        offset = jnp.where(edge, jnp.where(top, -3, 13), offset)
-        kind = jnp.where(top, 1, jnp.where(bottom, 2, 0))
-        start = pl.multiple_of(start, 8)
-        row = lax.broadcasted_iota(I32, (192, 80), 0)
-        select = (row - offset == place_out[kind]).astype(F32).astype(BF)
         for w in range(2):
-            j = jnp.where(inner, 1 + w, jnp.where(edge, 2 * ((u - 11) % 2) + w, 3 * w))
-            back = dot(select, att[80 * w : 80 * w + 80])
-            spot = (pl.ds(12 * j, 12), pl.ds(start, 16), slice(None))
-            acc[spot] = acc[spot] + back.reshape(12, 16, C)
+            j = jnp.where(edge == 1, v - 4, 3 * w)
+            add_back(
+                att,
+                j,
+                jnp.where(edge == 1, 32 * w, start),
+                jnp.where(edge == 1, 16 * w - 3, offset),
+                jnp.where(edge == 1, 1 + w, 0),
+            )
         return carry
 
-    lax.fori_loop(0, UNITS, unit, 0)
-
-    def finish(c, carry):
-        xo[c] = acc[c + 6].astype(BF)
-        return carry
-
-    def store(k):
-        part = pl.ds(9 * k, 9)
-        return pltpu.make_async_copy(xo.at[part], out.at[part], out_sem.at[k])
-
-    for k in range(4):
-        lax.fori_loop(9 * k, 9 * k + 9, finish, 0, unroll=3)
+    lax.fori_loop(0, 11, merged_unit, 0)
+    for k, first in ((0, 0), (2, COLS - 6)):
+        lax.fori_loop(first, first + 6, finish, 0, unroll=3)
         store(k).start()
 
     mirror_copy(zhi).wait_send()
@@ -590,7 +640,7 @@
             halo_copy(side, k).wait_send()
     lat_copy(True).wait_send()
     lat_copy(False).wait_send()
-    for k in range(4):
+    for k in range(3):
         store(k).wait()
 
 
@@ -630,6 +680,7 @@
             vm((4, 80, 128), BF),
             vm((80, 192), I32),
             vm((3, 192, 80), I32),
+            vm((2, 80, 128), F32),
             dma((6,)),
             dma((4,)),
             dma,

time: 137 us -> 130 us (0.949)
  Pallas kernels: 134 us -> 127 us
    pallas_call x1, Pallas kernels: 134 us -> 127 us  [local(): pl.pallas_call(functools.partial(kernel, nlat, nlon), out_shape=jax.Shape...]
where the time goes in v5:
time: 130 us
  Pallas kernels  127 us (98%)
  local copies, waits for them, and re-layouts  2.8 us (2%)
    pallas_call x1, Pallas kernels, local(): pl.pallas_call(functools.partial(kernel, nlat, nlon), out_shape=jax.Shape...  127 us
    unnamed x1, local copies, waits for them, and re-layouts  2.8 us

profile of v5, /device:TPU:72, one launch (start us, length us, event | category | flops | bytes accessed | tf_op | source)
XLA Modules:
  0.0 129.6 jit_solution(1287766810101799132)
XLA Ops:
  0.0 126.8 %shard_map.64 = bf16[36,48,512]{2,1,0:T(8,128)(2,1)} custom-call(bf16[36,48,512]{2,1,0:T(8,128)(2,1)} %bitcast.5, s32[36,48]{1,0:T(8,128)} %bitcast.6, f32[1,512]{1,0:T(1,128)} %bitcast.7, bf16[16,1536]{1,0:T(8,128)(2,1)} %wqkv.1, bf16[16,512]{1,0:T(8,128)(2,1)} %wproj.1, f32[16,72,72]{2,1,0:T(8,128)} %bias_hbm.1), custom_call_target="tpu_custom_call" | custom-call | flops 8000000000 | bytes 12000000 | tf_op jit(solution)/shard_map/pallas_call | solution.py:655
  126.8 2.8 %copy.8 = bf16[48,36,512]{2,0,1:T(8,128)(2,1)} copy(bf16[48,36,512]{2,0,1:T(8,128)(2,1)} %bitcast.4) | data formatting | bytes 3538944

commit v6 on v5

--- a/solution.py
+++ b/solution.py
@@ -93,10 +93,8 @@
     out_sem,
     z_send,
     z_recv,
-    line_send,
-    line_recv,
-    block_send,
-    block_recv,
+    plane_send,
+    plane_recv,
     sib_send,
     sib_recv,
     leg_send,
@@ -184,23 +182,23 @@
         below,
     )
     greeted = greeted + relays_here
-    greeted = greeted + tuple((lat, (y * nx + lax.rem(x + d, nx)) * 2 + zhi) for d in range(1, nx))
-    greeted = greeted + tuple((lat, (lax.rem(y + d, ny) * nx + x) * 2 + zhi) for d in range(1, ny))
     for there in greeted:
         pl.semaphore_signal(barrier, inc=1, device_id=there, device_id_type=MESH)
-    pl.semaphore_wait(barrier, len(greeted))
-
-    def plane_device(py, px):
-        return lat, (py * nx + px) * 2 + zhi
-
-    def at_x(d):
-        return lax.rem(x + d, nx)
-
-    def at_y(d):
-        return lax.rem(y + d, ny)
+
+    def greet(d, carry):
+        there = (lat, lax.rem(m + d, plane) * 2 + zhi)
+        pl.semaphore_signal(barrier, inc=1, device_id=there, device_id_type=MESH)
+        return carry
+
+    lax.fori_loop(1, plane, greet, 0)
+    pl.semaphore_wait(barrier, len(greeted) + plane - 1)
+
+    def shard_of(half, source, zh):
+        rows = pl.ds(zh * shard, shard)
+        return wbuf.at[pl.ds(2 * half, 2), source // nx, lax.rem(source, nx), rows, :]
 
     def mirror_copy(of):
-        part = wbuf.at[pl.ds(2 * core, 2), y, x, pl.ds(of * shard, shard), :]
+        part = shard_of(core, m, of)
         return pltpu.make_async_remote_copy(
             src_ref=part,
             dst_ref=part,
@@ -210,66 +208,39 @@
             device_id_type=MESH,
         )
 
-    def line_copy(a, d, owner):
-        py, px = (y, owner) if a == 0 else (owner, x)
-        part = wbuf.at[2 * core + a, py, px]
+    def plane_copy(k, d, source):
+        part = shard_of(core, source, zhi if k == 0 else 1 - zhi)
         return pltpu.make_async_remote_copy(
             src_ref=part,
             dst_ref=part,
-            send_sem=line_send.at[a, d],
-            recv_sem=line_recv.at[a, owner],
-            device_id=plane_device(y, at_x(d)) if a == 0 else plane_device(at_y(d), x),
+            send_sem=plane_send.at[k, d],
+            recv_sem=plane_recv.at[k, source],
+            device_id=(lat, lax.rem(m + d, plane) * 2 + zhi),
             device_id_type=MESH,
         )
 
-    def block_of(half, a, owner):
-        return wbuf.at[2 * half, owner] if a == 0 else wbuf.at[2 * half + 1, :, owner]
-
-    def block_copy(a, d, owner):
-        part = block_of(core, a, owner)
+    def sibling_copy(half, source):
+        part = wbuf.at[pl.ds(2 * half, 2), source // nx, lax.rem(source, nx)]
         return pltpu.make_async_remote_copy(
             src_ref=part,
             dst_ref=part,
-            send_sem=block_send.at[a, d],
-            recv_sem=block_recv.at[a, owner],
-            device_id=plane_device(at_y(d), x) if a == 0 else plane_device(y, at_x(d)),
-            device_id_type=MESH,
-        )
-
-    def sibling_copy(half, a, owner):
-        part = block_of(half, a, owner)
-        return pltpu.make_async_remote_copy(
-            src_ref=part,
-            dst_ref=part,
-            send_sem=sib_send.at[a, owner],
-            recv_sem=sib_recv.at[a, owner],
+            send_sem=sib_send.at[source],
+            recv_sem=sib_recv.at[source],
             device_id=(lat_sib, lon),
             device_id_type=MESH,
         )
 
-    first_axis = ((nx, x, at_x), (ny, y, at_y))
-    second_axis = ((ny, y, at_y), (nx, x, at_x))
-
-    def send_lines():
-        for a, (n, me, _) in enumerate(first_axis):
-            for d in range(1, n):
-                line_copy(a, d, me).start()
-
-    def send_blocks():
-        for a, (n, _, at) in enumerate(first_axis):
-            for d in range(1, n):
-                line_copy(a, d, at(d)).wait_recv()
-        for a, (n, me, _) in enumerate(second_axis):
-            for d in range(1, n):
-                block_copy(a, d, me).start()
-            sibling_copy(core, a, me).start()
-
-    def pass_on():
-        for d in range(1, max(nx, ny)):
-            for a, (n, _, at) in enumerate(second_axis):
-                if d < n:
-                    block_copy(a, d, at(d)).wait_recv()
-                    sibling_copy(core, a, at(d)).start()
+    def over_plane(first, body):
+        def step(d, carry):
+            body(d, lax.rem(m + d, plane))
+            return carry
+
+        lax.fori_loop(first, plane, step, 0)
+
+    def pass_on(d, source):
+        plane_copy(0, d, source).wait_recv()
+        plane_copy(1, d, source).wait_recv()
+        sibling_copy(core, source).start()
 
     for c in range(2):
 
@@ -326,9 +297,12 @@
     lab_send[...] = jnp.zeros_like(lab_send)
     lab_send[0, 0:6, 0:ROWS] = lab_own[COLS - 6 : COLS, :]
     lab_send[1, 0:6, 0:ROWS] = lab_own[0:6, :]
+    set_out(0)
     for side in range(2):
         label_copy(side).start()
-    set_out(0)
+    over_plane(1, lambda d, source: plane_copy(0, d, m).start())
+    set_out(1)
+    set_out(2)
 
     lane80 = lax.broadcasted_iota(I32, (80, 128), 1)
     for k in range(4):
@@ -355,12 +329,10 @@
 
     lax.fori_loop(0, COLS // 2, own_column, 0, unroll=2)
     mirror_copy(1 - zhi).wait_recv()
-    send_lines()
-    set_out(1)
+    over_plane(1, lambda d, source: plane_copy(1, d, m).start())
+    sibling_copy(core, m).start()
     lax.fori_loop(COLS // 2, COLS, own_column, 0, unroll=2)
-    send_blocks()
     forward(0)
-    set_out(2)
 
     def place_rows(count):
         half, c, r = token_parts(lax.broadcasted_iota(I32, (count, WIN), 0))
@@ -379,8 +351,6 @@
 
     lax.fori_loop(0, HEADS, bias_of, 0, unroll=4)
     forward(1)
-    pass_on()
-    forward(2)
 
     for side in range(2):
         label_copy(side).wait_recv()
@@ -401,6 +371,8 @@
         return carry
 
     lax.fori_loop(0, EXT, features, 0, unroll=4)
+    forward(2)
+    over_plane(1, pass_on)
 
     def start_and_offset(i):
         start = 8 * ((13 * i) // 16)
@@ -423,9 +395,7 @@
 
     lax.fori_loop(0, 7, gather_inner, 0)
 
-    for a, (n, _, at) in enumerate(second_axis):
-        for d in range(n):
-            sibling_copy(1 - core, a, at(d)).wait_recv()
+    over_plane(0, lambda d, source: sibling_copy(1 - core, source).wait_recv())
 
     def halo_chunk(k):
         row = (0, 32, 16)[k]
@@ -625,14 +595,9 @@
         store(k).start()
 
     mirror_copy(zhi).wait_send()
-    for a, (n, me, _) in enumerate(first_axis):
-        for d in range(1, n):
-            line_copy(a, d, me).wait_send()
-    for a, (n, me, at) in enumerate(second_axis):
-        for d in range(1, n):
-            block_copy(a, d, me).wait_send()
-        for d in range(n):
-            sibling_copy(core, a, at(d)).wait_send()
+    over_plane(1, lambda d, source: plane_copy(0, d, m).wait_send())
+    over_plane(1, lambda d, source: plane_copy(1, d, m).wait_send())
+    over_plane(0, lambda d, source: sibling_copy(core, source).wait_send())
     for side in range(2):
         label_copy(side).wait_send()
         for k in range(3):
@@ -685,12 +650,10 @@
             dma((4,)),
             dma,
             dma,
-            dma((2, nx)),
-            dma((2, nx)),
-            dma((2, nx)),
-            dma((2, nx)),
-            dma((2, nx)),
-            dma((2, nx)),
+            dma((2, plane)),
+            dma((2, plane)),
+            dma((plane,)),
+            dma((plane,)),
             dma((2, 3)),
             dma((2, 3)),
             dma((2, 3)),

time: 130 us -> 127 us (0.977)
  the two profiles are of different devices: /device:TPU:72 before, /device:TPU:24 now
where the time goes in v6:
time: 127 us; the launch traced here: 125 us
  Pallas kernels  122 us (96%)
  local copies, waits for them, and re-layouts  2.8 us (2%)
    pallas_call x1, Pallas kernels, local(): pl.pallas_call(functools.partial(kernel, nlat, nlon), out_shape=jax.Shape...  122 us
    unnamed x1, local copies, waits for them, and re-layouts  2.8 us

profile of v6, /device:TPU:24, one launch (start us, length us, event | category | flops | bytes accessed | tf_op | source)
XLA Modules:
  0.0 124.9 jit_solution(4505436939247484660)
XLA Ops:
  0.0 122.1 %shard_map.64 = bf16[36,48,512]{2,1,0:T(8,128)(2,1)} custom-call(bf16[36,48,512]{2,1,0:T(8,128)(2,1)} %bitcast.5, s32[36,48]{1,0:T(8,128)} %bitcast.6, f32[1,512]{1,0:T(1,128)} %bitcast.7, bf16[16,1536]{1,0:T(8,128)(2,1)} %wqkv.1, bf16[16,512]{1,0:T(8,128)(2,1)} %wproj.1, f32[16,72,72]{2,1,0:T(8,128)} %bias_hbm.1), custom_call_target="tpu_custom_call" | custom-call | flops 8000000000 | bytes 12000000 | tf_op jit(solution)/shard_map/pallas_call | solution.py:620
  122.1 2.8 %copy.8 = bf16[48,36,512]{2,0,1:T(8,128)(2,1)} copy(bf16[48,36,512]{2,0,1:T(8,128)(2,1)} %bitcast.4) | data formatting | bytes 3538944

commit v7 on v6

--- a/solution.py
+++ b/solution.py
@@ -93,6 +93,7 @@
     out_sem,
     z_send,
     z_recv,
+    fan_send,
     plane_send,
     plane_recv,
     sib_send,
@@ -133,6 +134,10 @@
         place = lax.rem(place + 2 * ring, ring)
         return lax.rem(place, zlo) * 2 + core, column * 2 + place // zlo
 
+    zedge = (1 - zhi) * (zlo - 1)
+    lat_edge = zedge * 2 + core
+    at_edge = lat == lat_edge
+
     above = chip_at(m, z + leg)
     below = chip_at(m, z - leg)
 
@@ -177,7 +182,7 @@
         (lat, lon_dn),
         (lat_up, lon),
         (lat_dn, lon),
-        (lat_mirror, lon_pair),
+        (jnp.where(at_edge, lat_mirror, lat_edge), jnp.where(at_edge, lon_pair, lon)),
         above,
         below,
     )
@@ -191,7 +196,7 @@
         return carry
 
     lax.fori_loop(1, plane, greet, 0)
-    pl.semaphore_wait(barrier, len(greeted) + plane - 1)
+    pl.semaphore_wait(barrier, len(greeted) - 1 + plane - 1 + zlo * at_edge.astype(I32))
 
     def shard_of(half, source, zh):
         rows = pl.ds(zh * shard, shard)
@@ -208,6 +213,17 @@
             device_id_type=MESH,
         )
 
+    def fan_copy(d):
+        part = shard_of(core, m, 1 - zhi)
+        return pltpu.make_async_remote_copy(
+            src_ref=part,
+            dst_ref=part,
+            send_sem=fan_send.at[d],
+            recv_sem=z_recv,
+            device_id=(lax.rem(zedge + d, zlo) * 2 + core, lon),
+            device_id_type=MESH,
+        )
+
     def plane_copy(k, d, source):
         part = shard_of(core, source, zhi if k == 0 else 1 - zhi)
         return pltpu.make_async_remote_copy(
@@ -241,15 +257,6 @@
         plane_copy(0, d, source).wait_recv()
         plane_copy(1, d, source).wait_recv()
         sibling_copy(core, source).start()
-
-    for c in range(2):
-
-        @pl.when(core == c)
-        def _():
-            for copy in quarters[c]:
-                copy.wait()
-
-    mirror_copy(zhi).start()
 
     def leg_copy(side, k):
         rows = pl.ds((0, 32, 16)[k], 16)
@@ -283,6 +290,20 @@
             leg_copy(side, k).wait_recv()
             halo_copy(side, k).start()
 
+    set_out(0)
+
+    for c in range(2):
+
+        @pl.when(core == c)
+        def _():
+            for copy in quarters[c]:
+                copy.wait()
+
+    @pl.when(at_edge)
+    def _():
+        mirror_copy(zhi).start()
+
+
     def label_copy(side):
         return pltpu.make_async_remote_copy(
             src_ref=lab_send.at[side],
@@ -297,7 +318,6 @@
     lab_send[...] = jnp.zeros_like(lab_send)
     lab_send[0, 0:6, 0:ROWS] = lab_own[COLS - 6 : COLS, :]
     lab_send[1, 0:6, 0:ROWS] = lab_own[0:6, :]
-    set_out(0)
     for side in range(2):
         label_copy(side).start()
     over_plane(1, lambda d, source: plane_copy(0, d, m).start())
@@ -329,6 +349,12 @@
 
     lax.fori_loop(0, COLS // 2, own_column, 0, unroll=2)
     mirror_copy(1 - zhi).wait_recv()
+
+    @pl.when(at_edge)
+    def _():
+        for d in range(1, zlo):
+            fan_copy(d).start()
+
     over_plane(1, lambda d, source: plane_copy(1, d, m).start())
     sibling_copy(core, m).start()
     lax.fori_loop(COLS // 2, COLS, own_column, 0, unroll=2)
@@ -408,7 +434,7 @@
                 xn[c + side * (EXT - 6), row : row + 16, 0:C] = normed_rows(x, gain[...])
             return carry
 
-        lax.fori_loop(0, 6, one, 0)
+        lax.fori_loop(0, 6, one, 0, unroll=3)
 
     def pack(row, offset):
         block = xn[:, row : row + 16, :].reshape(EXT * 16, WIDE).astype(BF)
@@ -594,7 +620,12 @@
         lax.fori_loop(first, first + 6, finish, 0, unroll=3)
         store(k).start()
 
-    mirror_copy(zhi).wait_send()
+    @pl.when(at_edge)
+    def _():
+        mirror_copy(zhi).wait_send()
+        for d in range(1, zlo):
+            fan_copy(d).wait_send()
+
     over_plane(1, lambda d, source: plane_copy(0, d, m).wait_send())
     over_plane(1, lambda d, source: plane_copy(1, d, m).wait_send())
     over_plane(0, lambda d, source: sibling_copy(core, source).wait_send())
@@ -650,6 +681,7 @@
             dma((4,)),
             dma,
             dma,
+            dma((nlat // 2,)),
             dma((2, plane)),
             dma((2, plane)),
             dma((plane,)),

time: 127 us -> 133 us (1.047)
  the two profiles are of different devices: /device:TPU:24 before, /device:TPU:169 now
where the time goes in v7:
time: 133 us
  Pallas kernels  130 us (98%)
  local copies, waits for them, and re-layouts  2.8 us (2%)
    pallas_call x1, Pallas kernels, local(): pl.pallas_call(functools.partial(kernel, nlat, nlon), out_shape=jax.Shape...  130 us
    unnamed x1, local copies, waits for them, and re-layouts  2.8 us

profile of v7, /device:TPU:169, one launch (start us, length us, event | category | flops | bytes accessed | tf_op | source)
XLA Modules:
  0.0 133.1 jit_solution(10631411220014517741)
XLA Ops:
  0.0 130.3 %shard_map.64 = bf16[36,48,512]{2,1,0:T(8,128)(2,1)} custom-call(bf16[36,48,512]{2,1,0:T(8,128)(2,1)} %bitcast.5, s32[36,48]{1,0:T(8,128)} %bitcast.6, f32[1,512]{1,0:T(1,128)} %bitcast.7, bf16[16,1536]{1,0:T(8,128)(2,1)} %wqkv.1, bf16[16,512]{1,0:T(8,128)(2,1)} %wproj.1, f32[16,72,72]{2,1,0:T(8,128)} %bias_hbm.1), custom_call_target="tpu_custom_call" | custom-call | flops 8000000000 | bytes 12000000 | tf_op jit(solution)/shard_map/pallas_call | solution.py:651
  130.3 2.8 %copy.8 = bf16[48,36,512]{2,0,1:T(8,128)(2,1)} copy(bf16[48,36,512]{2,0,1:T(8,128)(2,1)} %bitcast.4) | data formatting | bytes 3538944

commit v8 on v6

--- a/solution.py
+++ b/solution.py
@@ -301,8 +301,6 @@
     for side in range(2):
         label_copy(side).start()
     over_plane(1, lambda d, source: plane_copy(0, d, m).start())
-    set_out(1)
-    set_out(2)
 
     lane80 = lax.broadcasted_iota(I32, (80, 128), 1)
     for k in range(4):
@@ -331,6 +329,8 @@
     mirror_copy(1 - zhi).wait_recv()
     over_plane(1, lambda d, source: plane_copy(1, d, m).start())
     sibling_copy(core, m).start()
+    set_out(1)
+    set_out(2)
     lax.fori_loop(COLS // 2, COLS, own_column, 0, unroll=2)
     forward(0)
 
@@ -371,8 +371,8 @@
         return carry
 
     lax.fori_loop(0, EXT, features, 0, unroll=4)
+    over_plane(1, pass_on)
     forward(2)
-    over_plane(1, pass_on)
 
     def start_and_offset(i):
         start = 8 * ((13 * i) // 16)
@@ -408,7 +408,7 @@
                 xn[c + side * (EXT - 6), row : row + 16, 0:C] = normed_rows(x, gain[...])
             return carry
 
-        lax.fori_loop(0, 6, one, 0)
+        lax.fori_loop(0, 6, one, 0, unroll=3)
 
     def pack(row, offset):
         block = xn[:, row : row + 16, :].reshape(EXT * 16, WIDE).astype(BF)

time: 127 us -> 123 us (0.969)
  Pallas kernels: 122 us -> 118 us
    pallas_call x1, Pallas kernels: 122 us -> 118 us  [local(): pl.pallas_call(functools.partial(kernel, nlat, nlon), out_shape=jax.Shape...]
where the time goes in v8:
time: 123 us; the launch traced here: 121 us
  Pallas kernels  118 us (96%)
  local copies, waits for them, and re-layouts  2.8 us (2%)
    pallas_call x1, Pallas kernels, local(): pl.pallas_call(functools.partial(kernel, nlat, nlon), out_shape=jax.Shape...  118 us
    unnamed x1, local copies, waits for them, and re-layouts  2.8 us

profile of v8, /device:TPU:24, one launch (start us, length us, event | category | flops | bytes accessed | tf_op | source)
XLA Modules:
  0.0 120.7 jit_solution(1996333278334208519)
XLA Ops:
  0.0 117.9 %shard_map.64 = bf16[36,48,512]{2,1,0:T(8,128)(2,1)} custom-call(bf16[36,48,512]{2,1,0:T(8,128)(2,1)} %bitcast.5, s32[36,48]{1,0:T(8,128)} %bitcast.6, f32[1,512]{1,0:T(1,128)} %bitcast.7, bf16[16,1536]{1,0:T(8,128)(2,1)} %wqkv.1, bf16[16,512]{1,0:T(8,128)(2,1)} %wproj.1, f32[16,72,72]{2,1,0:T(8,128)} %bias_hbm.1), custom_call_target="tpu_custom_call" | custom-call | flops 8000000000 | bytes 12000000 | tf_op jit(solution)/shard_map/pallas_call | solution.py:620
  117.9 2.8 %copy.8 = bf16[48,36,512]{2,0,1:T(8,128)(2,1)} copy(bf16[48,36,512]{2,0,1:T(8,128)(2,1)} %bitcast.4) | data formatting | bytes 3538944
